TPU v7x, 128 devices: a whole 4x4x4 slice. The times are simulated.
128 devices in a mesh: gx: 4 (over x_hi, core), gy: 8 (over x_lo, y), gz: 4 (over z).
Axes of the slice: x: 4 (x_hi: 2, x_lo: 2; x = x_hi * 2 + x_lo), y: 4, z: 4, core: 2. Of those that a mesh axis runs over, the one named last changes fastest.
Arguments:
- conc: float32 [128, 512, 1024], P('gx', 'gy', 'gz'), may hold values from 0.2 to 1
- load: float32 [128, 512, 1024], P('gx', 'gy', 'gz'), may hold values from 0 to 1
- adj_conc: float32 [128, 512, 1024], P('gx', 'gy', 'gz'), may hold values from -6 to 6
- adj_load: float32 [128, 512, 1024], P('gx', 'gy', 'gz'), may hold values from -6 to 6
- vel_x: float32 [128, 512, 1024], P('gx', 'gy', 'gz'), may hold values from -0.03 to 0.03
- vel_y: float32 [128, 512, 1024], P('gx', 'gy', 'gz'), may hold values from -0.03 to 0.03
- vel_z: float32 [128, 512, 1024], P('gx', 'gy', 'gz'), may hold values from -0.03 to 0.03
- solid: int32 [128, 512, 1024], P('gx', 'gy', 'gz'), may hold values 0 or 1
- voxel_slot: int32 [128, 512, 1024], P('gx', 'gy', 'gz'), may hold values from 0 to 4095
- slot_grain: int32 [128, 4096], P(('gx', 'gy', 'gz')), may hold values from 0 to 262143, as said below
- grain_home: int32 [262144], replicated, may hold values from 0 to 262143, as said below
- rates: float32 [262144], P(('gx', 'gy', 'gz')), may hold values from 0.01 to 0.2
Outputs:
- adj_conc_start: float32 [128, 512, 1024], P('gx', 'gy', 'gz')
- adj_load_start: float32 [128, 512, 1024], P('gx', 'gy', 'gz')
- rate_grad: float32 [262144], P(('gx', 'gy', 'gz'))
Inputs may be any that keep to these rules, and one draw needn't show every extreme that they name: `slot_grain`: device block t's slots name grains t * 2048 to t * 2048 + 2 * 2048 - 1, taken modulo 262144, so a grain appears in the tables of neighbouring blocks. `grain_home`: A permutation of the 262144 places.
All inputs are finite; a program needn't handle non-finite values. No bound on the sum of `solid` on one device may be relied on, other than what follows from the above.
Results may differ from a plain program's by a relative error of at most 0.00013.
Values sent between devices are 32-bit elements; how exact they have to be, the bound alone decides.
A program may use at most 256 MiB of HBM per device.

v0:
```python
import jax
import jax.numpy as jnp
from jax import lax
from jax.sharding import PartitionSpec as P

dispersion = 0.06


def with_halo(block, sides, width):
    for axis, dim in sides:
        count = lax.axis_size(axis)
        forward = [(i, i + 1) for i in range(count - 1)]
        backward = [(target, source) for source, target in forward]
        low = lax.ppermute(
            lax.slice_in_dim(block, block.shape[dim] - width, None, axis=dim), axis, forward
        )
        high = lax.ppermute(lax.slice_in_dim(block, 0, width, axis=dim), axis, backward)
        block = jnp.concatenate([low, block, high], axis=dim)
    return block


def neighbour(values, dimension, offset):
    spans = [slice(1, -1), slice(1, -1), slice(1, -1)]
    length = values.shape[dimension]
    spans[dimension] = slice(1 + offset, length - 1 + offset)
    return values[tuple(spans)]


def forward(conc_ext, load, weight_ext, speeds, kvox):
    centre = neighbour(conc_ext, 0, 0)
    weight = neighbour(weight_ext, 0, 0)
    spread = jnp.zeros_like(centre)
    transport = jnp.zeros_like(centre)
    for dimension in range(3):
        speed_ext = speeds[dimension]
        spread = spread + weight * neighbour(weight_ext, dimension, 1) * (
            neighbour(conc_ext, dimension, 1) - centre
        )
        spread = spread + weight * neighbour(weight_ext, dimension, -1) * (
            neighbour(conc_ext, dimension, -1) - centre
        )
        speed = neighbour(speed_ext, 0, 0)
        before = neighbour(speed_ext, dimension, -1)
        upper = jnp.maximum(speed, 0.0) * centre + jnp.minimum(speed, 0.0) * neighbour(
            conc_ext, dimension, 1
        )
        lower = (
            jnp.maximum(before, 0.0) * neighbour(conc_ext, dimension, -1)
            + jnp.minimum(before, 0.0) * centre
        )
        transport = transport + (lower - upper)
    uptake = kvox * (centre / (1.0 + centre) - load)
    return (centre + dispersion * spread + transport - uptake, load + uptake)


def adjoint(adj_ext, adj_load, conc, load, weight_ext, speeds, kvox):
    centre = neighbour(adj_ext, 0, 0)
    weight = neighbour(weight_ext, 0, 0)
    spread = jnp.zeros_like(centre)
    transport = jnp.zeros_like(centre)
    for dimension in range(3):
        speed_ext = speeds[dimension]
        spread = spread + weight * neighbour(weight_ext, dimension, 1) * (
            neighbour(adj_ext, dimension, 1) - centre
        )
        spread = spread + weight * neighbour(weight_ext, dimension, -1) * (
            neighbour(adj_ext, dimension, -1) - centre
        )
        speed = neighbour(speed_ext, 0, 0)
        before = neighbour(speed_ext, dimension, -1)
        transport = transport + jnp.maximum(speed, 0.0) * (
            neighbour(adj_ext, dimension, 1) - centre
        )
        transport = transport + jnp.minimum(before, 0.0) * (
            centre - neighbour(adj_ext, dimension, -1)
        )
    differ = adj_load - centre
    denom = 1.0 + conc
    new_conc = centre + dispersion * spread + transport + kvox * differ / (denom * denom)
    new_load = adj_load - kvox * differ
    terms = (conc / denom - load) * differ
    return (new_conc, new_load, terms)


def per_device(
    conc,
    load,
    adj_conc,
    adj_load,
    vel_x,
    vel_y,
    vel_z,
    solid,
    voxel_slot,
    slot_grain,
    grain_home,
    rates,
):
    places = grain_home[slot_grain[0]]
    total_grains = grain_home.shape[0]
    rates_all = lax.all_gather(rates, ("gx", "gy", "gz"), axis=0, tiled=True)
    slot_rate = rates_all[places]
    slots = slot_grain.shape[1]
    lowest = 32
    highest = slots // lowest
    high_ids = jnp.arange(highest, dtype=jnp.int32)
    low_ids = jnp.arange(lowest, dtype=jnp.int32)
    label_blocks = voxel_slot.reshape(8, -1)
    rate_table = slot_rate.reshape(highest, lowest)

    def lookup(carry, block_labels):
        lower_hot = (block_labels[:, None] % lowest == low_ids[None, :]).astype(jnp.float32)
        candidates = jnp.dot(lower_hot, rate_table.T, precision=lax.Precision.HIGHEST)
        chosen = jnp.where(block_labels[:, None] // lowest == high_ids[None, :], candidates, 0.0)
        return (carry, jnp.sum(chosen, axis=1))

    unused_carry, voxel_rates = lax.scan(lookup, jnp.zeros((), jnp.float32), label_blocks)
    solid_float = solid.astype(jnp.float32)
    weight = 1.0 - 0.7 * solid_float
    kvox = solid_float * voxel_rates.reshape(voxel_slot.shape)
    stacked = jnp.stack([weight, vel_x, vel_y, vel_z, conc, adj_conc])
    extended = with_halo(stacked, (("gx", 1), ("gy", 2), ("gz", 3)), 1)
    speeds_near = (extended[1], extended[2], extended[3])
    conc_one, load_one = forward(extended[4], load, extended[0], speeds_near, kvox)
    adj_one, adj_load_one, late = adjoint(
        extended[5], adj_load, conc_one, load_one, extended[0], speeds_near, kvox
    )
    adj_wide = with_halo(adj_one, (("gx", 0), ("gy", 1), ("gz", 2)), 1)
    adj_start, adj_load_start, early = adjoint(
        adj_wide, adj_load_one, conc, load, extended[0], speeds_near, kvox
    )
    voxel_terms = solid_float * (early + late)
    term_blocks = voxel_terms.reshape(8, -1)

    def accumulate(totals, block):
        block_terms, block_labels = block
        upper_hot = (block_labels[:, None] // lowest == high_ids[None, :]).astype(jnp.float32)
        lower_hot = jnp.where(
            block_labels[:, None] % lowest == low_ids[None, :], block_terms[:, None], 0.0
        )
        product = jnp.einsum("nh,nl->hl", upper_hot, lower_hot, precision=lax.Precision.HIGHEST)
        return (totals + product, None)

    start_totals = jnp.zeros((highest, lowest), jnp.float32)
    slot_totals, unused = lax.scan(accumulate, start_totals, (term_blocks, label_blocks))
    dense = jnp.zeros((total_grains,), jnp.float32).at[places].add(slot_totals.reshape(-1))
    rate_grad = lax.psum_scatter(dense, ("gx", "gy", "gz"), scatter_dimension=0, tiled=True)
    return (adj_start, adj_load_start, rate_grad)


def solution(mesh):
    in_specs = (
        P("gx", "gy", "gz"),
        P("gx", "gy", "gz"),
        P("gx", "gy", "gz"),
        P("gx", "gy", "gz"),
        P("gx", "gy", "gz"),
        P("gx", "gy", "gz"),
        P("gx", "gy", "gz"),
        P("gx", "gy", "gz"),
        P("gx", "gy", "gz"),
        P(("gx", "gy", "gz"), None),
        P(),
        P(("gx", "gy", "gz")),
    )
    out_specs = (P("gx", "gy", "gz"), P("gx", "gy", "gz"), P(("gx", "gy", "gz")))
    return jax.shard_map(
        per_device, mesh=mesh, in_specs=in_specs, out_specs=out_specs, check_vma=False
    )
```

profile of v0, /device:TPU:1, one launch (start us, length us, event | category | flops | bytes accessed | tf_op | source)
XLA Modules:
  0.0 1057.4 jit_solution(3169149740342664255)
XLA Ops:
  16.1 4.5 copy-done.4
  20.6 6.0 collective-permute-start
  28.7 23.0 %gather_fusion = s32[4096]{0:T(1024)S(1)} fusion(s32[262144]{0:T(1024)S(1)} %copy-done, s32[4096]{0:T(1024)S(1)} %broadcast_clamp_fusion), kind=kCustom, calls=%fused_computation | custom fusion | bytes 49152 | tf_op jit(solution)/shard_map/gather | solution.py:99
  60.1 4.1 collective-permute-done.3
  64.2 10.6 %pad_maximum_fusion.1 = f32[6,34,66,256]{3,2,1,0:T(8,128)} fusion(f32[6,34,1,256]{3,2,1,0:T(1,128)S(1)} %collective-permute-done.3, f32[6,1,64,256]{3,2,1,0:T(8,128)S(1)} %collective-permute-done.1, f32[6,32,64,256]{3,2,1,0:T(8,128)} %copy-done.4, f32[6,1,64,256]{3,2,1,0:T(8,128)S(1)} %collective-permute-done, f32[6,34,1,256]{3,2,1,0:T(1,128)S(1)} %collective-permute-done.2), kind=kLoop, calls=%fused_computation.42 | loop fusion | flops 13787136 | bytes 27574272 | tf_op jit(solution)/shard_map/concatenate | solution.py:18
  74.8 12.6 %fusion.67 = (f32[6,34,66,1]{3,2,1,0:T(8,128)}, f32[6,34,66,1]{3,2,1,0:T(8,128)}) fusion(f32[6,34,66,256]{3,2,1,0:T(8,128)} %pad_maximum_fusion.1), kind=kLoop, calls=%fused_computation.150 | loop fusion | bytes 215424 | tf_op jit(solution)/shard_map/slice | solution.py:15
  87.4 5.1 copy.50
  95.8 5.8 copy.51
  105.0 4.8 copy.52
  109.8 5.4 copy.53
  115.2 23.2 %pad_maximum_fusion = f32[6,34,66,258]{3,2,1,0:T(8,128)} fusion(f32[6,34,66,1]{3,2,1,0:T(8,128)} %copy.53, f32[6,34,1,256]{3,2,1,0:T(1,128)S(1)} %collective-permute-done.3, f32[6,1,64,256]{3,2,1,0:T(8,128)S(1)} %copy-done.10, f32[6,32,64,256]{3,2,1,0:T(8,128)} %copy-done.4, f32[6,1,64,256]{3,2,1,0:T(8,128)S(1)} %collective-permute-done, ...), kind=kLoop, calls=%fused_computation.41 | loop fusion | flops 20842272 | bytes 27789696 | tf_op jit(solution)/shard_map/concatenate | solution.py:18
  138.4 15.7 %slice_bitcast_fusion.5 = (f32[34,66,258]{2,1,0:T(8,128)}, f32[34,66,258]{2,1,0:T(8,128)}, f32[34,66,258]{2,1,0:T(8,128)}, f32[34,66,258]{2,1,0:T(8,128)}, f32[34,66,258]{2,1,0:T(8,128)}, /*index=5*/f32[34,66,258]{2,1,0:T(8,128)}) fusion(f32[6,34,66,258]{3,2,1,0:T(8,128)} %pad_maximum_fusion), kind=kLoop, calls=%fused_computation.48 | loop fusion | bytes 27789696 | tf_op jit(solution)/shard_map/squeeze | solution.py:126
  154.1 169.8 %all-gather.2.cloned.1.call-done = f32[262144]{0:T(1024)} async-done(((f32[2048]{0:T(1024)}), f32[262144]{0:T(1024)}) %all-gather.2.cloned.1.call-update) | async-done | bytes 1048592 | tf_op jit(solution)/shard_map/all_gather | solution.py:101
  323.9 48.5 %gather_fusion.1 = f32[4096]{0:T(1024)S(1)} fusion(f32[262144]{0:T(1024)} %all-gather.2.cloned.1.call-done, s32[4096]{0:T(1024)S(1)} %broadcast_clamp_fusion.1), kind=kCustom, calls=%fused_computation.1 | custom fusion | bytes 49152 | tf_op jit(solution)/shard_map/gather | solution.py:102
  372.4 188.4 %while.26 = (s32[]{:T(128)}, f32[8,65536]{1,0:T(8,128)}, s32[8,65536]{1,0:T(8,128)S(1)}, f32[128,32]{1,0:T(8,128)S(1)}, s32[]{:T(128)}, /*index=5*/s32[]{:T(128)}) while((s32[]{:T(128)}, f32[8,65536]{1,0:T(8,128)}, s32[8,65536]{1,0:T(8,128)S(1)}, f32[128,32]{1,0:T(8,128)S(1)}, s32[]{:T(128)}, /*index=5*/s32[]{:T(128)}) %tuple.78), condition=%wide.region_2.3_spmd.clone, body=%wide.region_0.2_spmd.clone.sunk | while | flops 3249668096 | bytes 2637901 | solution.py:117
  372.9 17.1 %fusion.83 = f32[65536]{0:T(1024)S(1)} fusion(f32[128,32]{1,0:T(8,128)S(1)} %get-tuple-element.313, s32[65536]{0:T(1024)S(1)} %get-tuple-element.290, s32[65536]{0:T(1024)S(1)} %get-tuple-element.291), kind=kOutput, calls=%fused_computation.10.clone.1 | convolution fusion | flops 3248422912 | bytes 802816 | tf_op jit(solution)/shard_map/while/body/eval_jaxpr/dot_general | solution.py:113
  390.0 6.0 dynamic_update_slice.9
  396.4 17.1 %fusion.83 = f32[65536]{0:T(1024)S(1)} fusion(f32[128,32]{1,0:T(8,128)S(1)} %get-tuple-element.313, s32[65536]{0:T(1024)S(1)} %get-tuple-element.290, s32[65536]{0:T(1024)S(1)} %get-tuple-element.291), kind=kOutput, calls=%fused_computation.10.clone.1 | convolution fusion | flops 3248422912 | bytes 802816 | tf_op jit(solution)/shard_map/while/body/eval_jaxpr/dot_general | solution.py:113
  413.5 6.0 dynamic_update_slice.9
  420.0 17.1 %fusion.83 = f32[65536]{0:T(1024)S(1)} fusion(f32[128,32]{1,0:T(8,128)S(1)} %get-tuple-element.313, s32[65536]{0:T(1024)S(1)} %get-tuple-element.290, s32[65536]{0:T(1024)S(1)} %get-tuple-element.291), kind=kOutput, calls=%fused_computation.10.clone.1 | convolution fusion | flops 3248422912 | bytes 802816 | tf_op jit(solution)/shard_map/while/body/eval_jaxpr/dot_general | solution.py:113
  437.1 6.0 dynamic_update_slice.9
  443.5 17.1 %fusion.83 = f32[65536]{0:T(1024)S(1)} fusion(f32[128,32]{1,0:T(8,128)S(1)} %get-tuple-element.313, s32[65536]{0:T(1024)S(1)} %get-tuple-element.290, s32[65536]{0:T(1024)S(1)} %get-tuple-element.291), kind=kOutput, calls=%fused_computation.10.clone.1 | convolution fusion | flops 3248422912 | bytes 802816 | tf_op jit(solution)/shard_map/while/body/eval_jaxpr/dot_general | solution.py:113
  460.6 6.0 dynamic_update_slice.9
  467.0 17.1 %fusion.83 = f32[65536]{0:T(1024)S(1)} fusion(f32[128,32]{1,0:T(8,128)S(1)} %get-tuple-element.313, s32[65536]{0:T(1024)S(1)} %get-tuple-element.290, s32[65536]{0:T(1024)S(1)} %get-tuple-element.291), kind=kOutput, calls=%fused_computation.10.clone.1 | convolution fusion | flops 3248422912 | bytes 802816 | tf_op jit(solution)/shard_map/while/body/eval_jaxpr/dot_general | solution.py:113
  484.2 6.0 dynamic_update_slice.9
  490.6 17.1 %fusion.83 = f32[65536]{0:T(1024)S(1)} fusion(f32[128,32]{1,0:T(8,128)S(1)} %get-tuple-element.313, s32[65536]{0:T(1024)S(1)} %get-tuple-element.290, s32[65536]{0:T(1024)S(1)} %get-tuple-element.291), kind=kOutput, calls=%fused_computation.10.clone.1 | convolution fusion | flops 3248422912 | bytes 802816 | tf_op jit(solution)/shard_map/while/body/eval_jaxpr/dot_general | solution.py:113
  507.7 6.0 dynamic_update_slice.9
  514.1 17.1 %fusion.83 = f32[65536]{0:T(1024)S(1)} fusion(f32[128,32]{1,0:T(8,128)S(1)} %get-tuple-element.313, s32[65536]{0:T(1024)S(1)} %get-tuple-element.290, s32[65536]{0:T(1024)S(1)} %get-tuple-element.291), kind=kOutput, calls=%fused_computation.10.clone.1 | convolution fusion | flops 3248422912 | bytes 802816 | tf_op jit(solution)/shard_map/while/body/eval_jaxpr/dot_general | solution.py:113
  531.2 6.0 dynamic_update_slice.9
  537.7 17.1 %fusion.83 = f32[65536]{0:T(1024)S(1)} fusion(f32[128,32]{1,0:T(8,128)S(1)} %get-tuple-element.313, s32[65536]{0:T(1024)S(1)} %get-tuple-element.290, s32[65536]{0:T(1024)S(1)} %get-tuple-element.291), kind=kOutput, calls=%fused_computation.10.clone.1 | convolution fusion | flops 3248422912 | bytes 802816 | tf_op jit(solution)/shard_map/while/body/eval_jaxpr/dot_general | solution.py:113
  554.8 6.0 dynamic_update_slice.9
  564.8 34.3 %add_subtract_fusion = (f32[32,64,256]{2,1,0:T(8,128)}, f32[32,64,256]{2,1,0:T(8,128)}) fusion(f32[34,66,258]{2,1,0:T(8,128)} %get-tuple-element.223, f32[34,66,258]{2,1,0:T(8,128)} %get-tuple-element.224, f32[34,66,258]{2,1,0:T(8,128)} %get-tuple-element.225, f32[34,66,258]{2,1,0:T(8,128)} %get-tuple-element.226, f32[32,64,256]{2,1,0:T(8,128)} %param.17, ...), kind=kLoop, calls=%fused_computation.128 | loop fusion | flops 35651584 | bytes 52428800 | tf_op jit(solution)/shard_map/sub | solution.py:53
  599.1 17.1 %fusion.29 = (f32[32,64,256]{2,1,0:T(8,128)}, f32[32,64,256]{2,1,0:T(8,128)}) fusion(f32[32,64,256]{2,1,0:T(8,128)} %get-tuple-element.216, f32[32,64,256]{2,1,0:T(8,128)} %param.17, f32[32,64,256]{2,1,0:T(8,128)} %param.16, s32[32,64,256]{2,1,0:T(8,128)} %param.23, f32[32,64,256]{2,1,0:T(8,128)} %param.19, f32[32,64,256]{2,1,0:T(8,128)} %get-tuple-element.217, ...), kind=kLoop, calls=%fused_computation.60 | loop fusion | flops 36175872 | bytes 60817408 | tf_op jit(solution)/shard_map/mul | solution.py:132
  619.1 5.1 collective-permute-start.7
  633.1 227.2 %while.27 = (s32[]{:T(128)}, f32[128,32]{0,1:T(8,128)S(1)}, s32[8,65536]{1,0:T(8,128)}, f32[8,65536]{1,0:T(8,128)}, s32[]{:T(128)}, /*index=5*/s32[]{:T(128)}) while((s32[]{:T(128)}, f32[128,32]{0,1:T(8,128)S(1)}, s32[8,65536]{1,0:T(8,128)}, f32[8,65536]{1,0:T(8,128)}, s32[]{:T(128)}, /*index=5*/s32[]{:T(128)}) %tuple.88), condition=%wide.region_4.5_spmd.clone, body=%wide.region_3.4_spmd.clone.sunk | while | flops 3235061760 | bytes 19431512 | solution.py:145
  640.7 20.8 %fusion.86 = f32[128,32]{0,1:T(8,128)S(1)} fusion(s32[65536]{0:T(1024)S(1)} %get-tuple-element.296, f32[128,32]{0,1:T(8,128)S(1)} %get-tuple-element.323, pred[]{:T(512)S(6)} %compare.31, f32[65536,32]{0,1:T(8,128)} %fusion.85), kind=kOutput, calls=%fused_computation.29.clone.3 | convolution fusion | flops 3229622272 | bytes 8683521 | tf_op jit(solution)/shard_map/while/body/eval_jaxpr/nh,nl->hl/dot_general | solution.py:141
  669.1 20.8 %fusion.86 = f32[128,32]{0,1:T(8,128)S(1)} fusion(s32[65536]{0:T(1024)S(1)} %get-tuple-element.296, f32[128,32]{0,1:T(8,128)S(1)} %get-tuple-element.323, pred[]{:T(512)S(6)} %compare.31, f32[65536,32]{0,1:T(8,128)} %fusion.85), kind=kOutput, calls=%fused_computation.29.clone.3 | convolution fusion | flops 3229622272 | bytes 8683521 | tf_op jit(solution)/shard_map/while/body/eval_jaxpr/nh,nl->hl/dot_general | solution.py:141
  697.5 20.8 %fusion.86 = f32[128,32]{0,1:T(8,128)S(1)} fusion(s32[65536]{0:T(1024)S(1)} %get-tuple-element.296, f32[128,32]{0,1:T(8,128)S(1)} %get-tuple-element.323, pred[]{:T(512)S(6)} %compare.31, f32[65536,32]{0,1:T(8,128)} %fusion.85), kind=kOutput, calls=%fused_computation.29.clone.3 | convolution fusion | flops 3229622272 | bytes 8683521 | tf_op jit(solution)/shard_map/while/body/eval_jaxpr/nh,nl->hl/dot_general | solution.py:141
  726.0 20.8 %fusion.86 = f32[128,32]{0,1:T(8,128)S(1)} fusion(s32[65536]{0:T(1024)S(1)} %get-tuple-element.296, f32[128,32]{0,1:T(8,128)S(1)} %get-tuple-element.323, pred[]{:T(512)S(6)} %compare.31, f32[65536,32]{0,1:T(8,128)} %fusion.85), kind=kOutput, calls=%fused_computation.29.clone.3 | convolution fusion | flops 3229622272 | bytes 8683521 | tf_op jit(solution)/shard_map/while/body/eval_jaxpr/nh,nl->hl/dot_general | solution.py:141
  754.4 20.8 %fusion.86 = f32[128,32]{0,1:T(8,128)S(1)} fusion(s32[65536]{0:T(1024)S(1)} %get-tuple-element.296, f32[128,32]{0,1:T(8,128)S(1)} %get-tuple-element.323, pred[]{:T(512)S(6)} %compare.31, f32[65536,32]{0,1:T(8,128)} %fusion.85), kind=kOutput, calls=%fused_computation.29.clone.3 | convolution fusion | flops 3229622272 | bytes 8683521 | tf_op jit(solution)/shard_map/while/body/eval_jaxpr/nh,nl->hl/dot_general | solution.py:141
  782.8 20.8 %fusion.86 = f32[128,32]{0,1:T(8,128)S(1)} fusion(s32[65536]{0:T(1024)S(1)} %get-tuple-element.296, f32[128,32]{0,1:T(8,128)S(1)} %get-tuple-element.323, pred[]{:T(512)S(6)} %compare.31, f32[65536,32]{0,1:T(8,128)} %fusion.85), kind=kOutput, calls=%fused_computation.29.clone.3 | convolution fusion | flops 3229622272 | bytes 8683521 | tf_op jit(solution)/shard_map/while/body/eval_jaxpr/nh,nl->hl/dot_general | solution.py:141
  811.2 20.8 %fusion.86 = f32[128,32]{0,1:T(8,128)S(1)} fusion(s32[65536]{0:T(1024)S(1)} %get-tuple-element.296, f32[128,32]{0,1:T(8,128)S(1)} %get-tuple-element.323, pred[]{:T(512)S(6)} %compare.31, f32[65536,32]{0,1:T(8,128)} %fusion.85), kind=kOutput, calls=%fused_computation.29.clone.3 | convolution fusion | flops 3229622272 | bytes 8683521 | tf_op jit(solution)/shard_map/while/body/eval_jaxpr/nh,nl->hl/dot_general | solution.py:141
  839.6 20.8 %fusion.86 = f32[128,32]{0,1:T(8,128)S(1)} fusion(s32[65536]{0:T(1024)S(1)} %get-tuple-element.296, f32[128,32]{0,1:T(8,128)S(1)} %get-tuple-element.323, pred[]{:T(512)S(6)} %compare.31, f32[65536,32]{0,1:T(8,128)} %fusion.85), kind=kOutput, calls=%fused_computation.29.clone.3 | convolution fusion | flops 3229622272 | bytes 8683521 | tf_op jit(solution)/shard_map/while/body/eval_jaxpr/nh,nl->hl/dot_general | solution.py:141
  867.3 4.0 collective-permute-start.11
  871.3 5.6 multiply_subtract_fusion
  877.1 23.1 %scatter_custom_fusion = f32[262144]{0:T(1024)} fusion(s32[4096]{0:T(1024)} %bitcast.52, f32[4096]{0:T(1024)S(1)} %reshape.283, f32[]{:T(128)} %constant.129.clone.1), kind=kCustom, calls=%fused_computation.138 | custom fusion | flops 4096 | bytes 1049088 | tf_op jit(solution)/shard_map/scatter-add | solution.py:146
  903.3 31.4 %fusion.31 = f32[32,64,256]{2,1,0:T(8,128)} fusion(f32[32,64,256]{2,1,0:T(8,128)} %param.16, f32[32,64,256]{2,1,0:T(8,128)S(1)} %copy-done.6, f32[34,1,256]{2,1,0:T(1,128)S(1)} %collective-permute-done.8, f32[1,64,256]{2,1,0:T(8,128)S(1)} %collective-permute-done.6, f32[1,64,256]{2,1,0:T(8,128)S(1)} %collective-permute-done.7, ...), kind=kLoop, calls=%fused_computation.62 | loop fusion | flops 38273024 | bytes 40064544 | tf_op jit(solution)/shard_map/add | solution.py:79
  934.7 114.5 %all-reduce.3.cloned.1.call-done = f32[262144]{0:T(1024)} async-done(((f32[262144]{0:T(1024)}), f32[262144]{0:T(1024)}) %all-reduce.3.cloned.1.call-update) | async-done | bytes 1048592
  (134 shorter events, 117.4 us)
Async XLA Ops:
  7.2 21.6 %copy-start = (s32[262144]{0:T(1024)S(1)}, s32[262144]{0:T(1024)}, u32[]{:S(2)}) copy-start(s32[262144]{0:T(1024)} %param.26) | copy-start | bytes 3145732
  7.2 2.3 copy-start.11
  7.2 316.7 %all-gather.2.cloned.1.call-start = ((), (), s32[]{:S(2)}) async-start(), calls=%async_computation | async-start | bytes 1056768 | tf_op jit(solution)/shard_map/all_gather | solution.py:101
  9.5 1.6 copy-start.12
  11.1 1.6 copy-start.13
  12.7 1.6 copy-start.7
  14.3 1.6 copy-start.14
  15.9 12.8 %copy-start.16 = (s32[1,4096]{1,0:T(1,128)S(1)}, s32[1,4096]{1,0:T(1,128)}, u32[]{:S(2)}) copy-start(s32[1,4096]{1,0:T(1,128)} %param.25) | copy-start | bytes 49156
  16.1 4.5 copy-start.4
  20.6 31.2 %collective-permute-start = (f32[6,1,64,256]{3,2,1,0:T(8,128)S(1)}, f32[6,1,64,256]{3,2,1,0:T(8,128)S(1)}, u32[]{:S(2)}, u32[]{:S(2)}) collective-permute-start(f32[6,1,64,256]{3,2,1,0:T(8,128)S(1)} %get-tuple-element.232), channel_id=1, source_target_pairs={{0,32},{32,64},{64,96},{1,33},{33,65},{65,97},{2,34},{34,66},{66,9... | collective-permute-start | bytes 1179656 | tf_op jit(solution)/shard_map/ppermute | solution.py:14
  26.7 25.1 %collective-permute-start.1 = (f32[6,1,64,256]{3,2,1,0:T(8,128)S(1)}, f32[6,1,64,256]{3,2,1,0:T(8,128)S(1)}, u32[]{:S(2)}, u32[]{:S(2)}) collective-permute-start(f32[6,1,64,256]{3,2,1,0:T(8,128)S(1)} %get-tuple-element.233), channel_id=1, source_target_pairs={{32,0},{64,32},{96,64},{33,1},{65,33},{97,65},{34,2},{66,34},{98,6... | collective-permute-start | bytes 1179656 | tf_op jit(solution)/shard_map/ppermute | solution.py:17
  28.6 1020.6 %all-reduce.3.cloned.1.call-start = ((), (), s32[]{:S(2)}) async-start(), calls=%async_computation.1 | async-start | bytes 2097152
  51.8 12.4 %copy-start.9 = (f32[6,1,64,256]{3,2,1,0:T(8,128)}, f32[6,1,64,256]{3,2,1,0:T(8,128)S(1)}, u32[]{:S(2)}) copy-start(f32[6,1,64,256]{3,2,1,0:T(8,128)S(1)} %collective-permute-done.1) | copy-start | bytes 1179652
  54.2 5.9 collective-permute-start.2
  57.4 6.8 collective-permute-start.3
  58.7 44.3 %copy-start.15 = (s32[4096,1]{0,1:T(1,128)}, s32[4096,1]{0,1:T(1,128)S(1)}, u32[]{:S(2)}) copy-start(s32[4096,1]{0,1:T(1,128)S(1)} %compare_select_fusion) | copy-start | bytes 49156
  92.5 12.5 %collective-permute-start.4 = (f32[6,34,66,1]{2,3,1,0:T(1,128)S(1)}, f32[6,34,66,1]{2,3,1,0:T(1,128)S(1)}, u32[]{:S(2)}, u32[]{:S(2)}) collective-permute-start(f32[6,34,66,1]{2,3,1,0:T(1,128)S(1)} %copy.50), channel_id=1, source_target_pairs={{0,1},{1,2},{2,3},{4,5},{5,6},{6,7},{8,9},{9,10},{10,11},{12,13},{... | collective-permute-start | bytes 161576 | tf_op jit(solution)/shard_map/ppermute | solution.py:14
  101.6 8.2 collective-permute-start.5
  109.8 5.4 copy-start.10
  560.8 4.0 copy-start.8
  564.8 34.3 %copy-start.2 = (f32[34,66,258]{2,1,0:T(8,128)S(1)}, f32[34,66,258]{2,1,0:T(8,128)}, u32[]{:S(2)}) copy-start(f32[34,66,258]{2,1,0:T(8,128)} %get-tuple-element.227) | copy-start | bytes 6947428
  564.8 34.3 %copy-start.3 = (f32[34,66,258]{2,1,0:T(8,128)S(1)}, f32[34,66,258]{2,1,0:T(8,128)}, u32[]{:S(2)}) copy-start(f32[34,66,258]{2,1,0:T(8,128)} %get-tuple-element.222) | copy-start | bytes 6947428
  564.8 34.3 %copy-start.5 = (f32[34,66,258]{2,1,0:T(8,128)S(1)}, f32[34,66,258]{2,1,0:T(8,128)}, u32[]{:S(2)}) copy-start(f32[34,66,258]{2,1,0:T(8,128)} %get-tuple-element.223) | copy-start | bytes 6947428
  617.1 10.6 %collective-permute-start.6 = (f32[1,64,256]{2,1,0:T(8,128)S(1)}, f32[1,64,256]{2,1,0:T(8,128)S(1)}, u32[]{:S(2)}, u32[]{:S(2)}) collective-permute-start(f32[1,64,256]{2,1,0:T(8,128)S(1)} %get-tuple-element.239), channel_id=1, source_target_pairs={{32,0},{64,32},{96,64},{33,1},{65,33},{97,65},{34,2},{66,34},{98,6... | collective-permute-start | bytes 196616 | tf_op jit(solution)/shard_map/ppermute | solution.py:17
  619.1 8.7 collective-permute-start.7
  624.2 3.5 copy-start.6
  627.8 232.5 %collective-permute-start.8 = (f32[34,1,256]{2,1,0:T(1,128)S(1)}, f32[34,1,256]{2,1,0:T(1,128)S(1)}, u32[]{:S(2)}, u32[]{:S(2)}) collective-permute-start(f32[34,1,256]{2,1,0:T(1,128)S(1)} %get-tuple-element.237), channel_id=1, source_target_pairs={{4,0},{8,4},{12,8},{16,12},{20,16},{24,20},{28,24},{5,1},{9,5},{13... | collective-permute-start | bytes 104456 | tf_op jit(solution)/shard_map/ppermute | solution.py:17
  629.1 231.2 %collective-permute-start.9 = (f32[34,1,256]{2,1,0:T(1,128)S(1)}, f32[34,1,256]{2,1,0:T(1,128)S(1)}, u32[]{:S(2)}, u32[]{:S(2)}) collective-permute-start(f32[34,1,256]{2,1,0:T(1,128)S(1)} %get-tuple-element.236), channel_id=1, source_target_pairs={{0,4},{4,8},{8,12},{12,16},{16,20},{20,24},{24,28},{1,5},{5,9},{9,... | collective-permute-start | bytes 104456 | tf_op jit(solution)/shard_map/ppermute | solution.py:14
  864.3 35.9 %collective-permute-start.10 = (f32[34,66,1]{1,2,0:T(1,128)S(1)}, f32[34,66,1]{1,2,0:T(1,128)S(1)}, u32[]{:S(2)}, u32[]{:S(2)}) collective-permute-start(f32[34,66,1]{1,2,0:T(1,128)S(1)} %copy.54), channel_id=1, source_target_pairs={{1,0},{2,1},{3,2},{5,4},{6,5},{7,6},{9,8},{10,9},{11,10},{13,12},{... | collective-permute-start | bytes 26936 | tf_op jit(solution)/shard_map/ppermute | solution.py:17
  867.3 34.4 %collective-permute-start.11 = (f32[34,66,1]{1,2,0:T(1,128)S(1)}, f32[34,66,1]{1,2,0:T(1,128)S(1)}, u32[]{:S(2)}, u32[]{:S(2)}) collective-permute-start(f32[34,66,1]{1,2,0:T(1,128)S(1)} %copy.56), channel_id=1, source_target_pairs={{0,1},{1,2},{2,3},{4,5},{5,6},{6,7},{8,9},{9,10},{10,11},{12,13},{... | collective-permute-start | bytes 26936 | tf_op jit(solution)/shard_map/ppermute | solution.py:14
  903.3 147.2 %copy-start.1 = (s32[262144]{0:T(1024)S(1)}, s32[262144]{0:T(1024)}, u32[]{:S(2)}) copy-start(s32[262144]{0:T(1024)} %param.26) | copy-start | bytes 3145732
Sparse Core Ops, SparseCore 0:
  28.8 295.0 all-gather.1
  900.3 148.8 all-reduce.2
where the time goes:
time: 1060 us
  matrix products  303 us (29%)
  waiting for transfers between devices  290 us (27%)
  local copies, waits for them, and re-layouts  231 us (22%)
  other arithmetic  184 us (17%)
  starting transfers between devices  34.9 us (3%)
  between operations  14.5 us (1%)
    all_gather x1, waiting for transfers between devices, per_device(): rates_all = lax.all_gather(rates, ('gx', 'gy', 'gz'), axis=0, tiled=True)  170 us
    dot_general x8, matrix products, accumulate(): jnp.einsum('nh,nl->hl', upper_hot, lower_hot, precision=lax.Precision.HIG...  166 us
    dot_general x8, matrix products, lookup(): jnp.dot(lower_hot, rate_table.T, precision=lax.Precision.HIGHEST)  137 us
    unnamed x3, waiting for transfers between devices  115 us
    gather x1, local copies, waits for them, and re-layouts, per_device(): slot_rate = rates_all[places]  48.5 us
    dynamic_update_slice x8, local copies, waits for them, and re-layouts, per_device(): lax.scan(lookup, jnp.zeros((), jnp.float32), label_blocks)  48.1 us
    sub x1, other arithmetic, forward(): return (centre + dispersion * spread + transport - uptake, load + uptake)  34.3 us
    concatenate x4, other arithmetic, with_halo(): block = jnp.concatenate([low, block, high], axis=dim)  34.1 us
  transfers between devices with their start and end apart: 14, of which 4 were waited for; matrix products, arithmetic and copies ran while one was open for 38% of the time, Pallas kernels for 0%

commit v1 on v0

v1 whole, which is shorter than its diff:
```python
import functools

import jax
import jax.numpy as jnp
from jax import lax
from jax.experimental import pallas as pl
from jax.experimental.pallas import tpu as pltpu
from jax.sharding import PartitionSpec as P

f32, bf16, i32 = jnp.float32, jnp.bfloat16, jnp.int32
MESH = pl.DeviceIdType.MESH
ANY = pl.BlockSpec(memory_space=pl.ANY)
dispersion = 0.06
rate_step = 0.2 / 65535.0
CX, CY, CZ = 32, 64, 256


def greet():
    barrier = pltpu.get_barrier_semaphore()
    for axis, count in (("gx", 4), ("gy", 8), ("gz", 4)):
        me = lax.axis_index(axis)
        for o in range(1, count):
            pl.semaphore_signal(
                barrier, inc=1, device_id={axis: lax.rem(me + o, count)}, device_id_type=MESH
            )
    pl.semaphore_wait(barrier, 13)


def gather_faces(
    conc, adj, vx, vy, vz, solid, rates,
    xlo, xlo_s, xhi, xhi_s, ylo, yhi, zlo, zhi, yown, zown, rall,
    ybuf, ysol, zbuf, zsol, yfwd, ybwd, zfwd, zbwd, lsem, rsem, osem, ssem, dsem,
):
    gx, gy, gz = (lax.axis_index(a) for a in ("gx", "gy", "gz"))
    xh, core = gx // 2, lax.rem(gx, 2)
    local = []
    pairs = ((conc, CY - 8), (adj, CY - 8), (vy, CY - 8), (conc, 0), (adj, 0))
    for k, (ref, start) in enumerate(pairs):
        local.append(pltpu.make_async_copy(ref.at[:, start:start + 8, :], ybuf.at[k], lsem.at[k]))
    for k, start in enumerate((CY - 8, 0)):
        local.append(pltpu.make_async_copy(solid.at[:, start:start + 8, :], ysol.at[k], lsem.at[5 + k]))
    pairs = ((conc, CZ - 128), (adj, CZ - 128), (vz, CZ - 128), (conc, 0), (adj, 0))
    for k, (ref, start) in enumerate(pairs):
        local.append(pltpu.make_async_copy(ref.at[:, :, start:start + 128], zbuf.at[k], lsem.at[7 + k]))
    for k, start in enumerate((CZ - 128, 0)):
        local.append(pltpu.make_async_copy(solid.at[:, :, start:start + 128], zsol.at[k], lsem.at[12 + k]))
    for copy in local:
        copy.start()
    mine = pltpu.make_async_copy(rates, rall.at[xh, core, gy, gz], osem.at[0])
    mine.start()
    greet()

    started = []

    def send(src, dst, where):
        k = len(started)
        copy = pltpu.make_async_remote_copy(
            src_ref=src, dst_ref=dst, send_sem=ssem.at[k], recv_sem=rsem.at[k],
            device_id=where, device_id_type=MESH,
        )
        copy.start()
        started.append(copy)
        return copy

    first = send(rates, rall.at[xh, core, gy, gz], {"gx": gx + 2 - 4 * xh})
    right, left = {"gx": lax.rem(gx + 1, 4)}, {"gx": lax.rem(gx + 3, 4)}
    faces = []
    for k, ref in enumerate((conc, adj, vx)):
        faces.append(send(ref.at[CX - 1], xlo.at[k], right))
    faces.append(send(solid.at[CX - 1], xlo_s, right))
    for k, ref in enumerate((conc, adj)):
        faces.append(send(ref.at[0], xhi.at[k], left))
    faces.append(send(solid.at[0], xhi_s, left))

    for copy in local[:7]:
        copy.wait()

    def rows(x, carry):
        at = pl.ds(x, 1)
        for k in range(3):
            yfwd[k, at, :] = ybuf[k, x, 7:8, :]
        yfwd[3, at, :] = 1.0 - 0.7 * ysol[0, x, 7:8, :].astype(f32)
        for k in range(2):
            ybwd[k, at, :] = ybuf[3 + k, x, 0:1, :]
        ybwd[2, at, :] = 1.0 - 0.7 * ysol[1, x, 0:1, :].astype(f32)
        return carry

    lax.fori_loop(0, CX, rows, 0)
    faces.append(send(yfwd, ylo, {"gy": lax.rem(gy + 1, 8)}))
    faces.append(send(ybwd, yhi, {"gy": lax.rem(gy + 7, 8)}))
    keep_y = pltpu.make_async_copy(ybwd, yown, osem.at[1])
    keep_y.start()

    mine.wait()
    first.wait_recv()
    second = [
        send(rall.at[:, core, gy, gz], rall.at[:, core, gy, gz], {"gz": lax.rem(gz + o, 4)})
        for o in range(1, 4)
    ]

    for copy in local[7:]:
        copy.wait()
    lane = lax.broadcasted_iota(i32, (CY, 128), 1)

    def columns(x, carry):
        fwd, bwd = carry
        for k in range(3):
            fwd = jnp.where(lane == x + 32 * k, zbuf[k, x][:, 127:128], fwd)
        fwd = jnp.where(lane == x + 96, 1.0 - 0.7 * zsol[0, x][:, 127:128].astype(f32), fwd)
        for k in range(2):
            bwd = jnp.where(lane == x + 32 * k, zbuf[3 + k, x][:, 0:1], bwd)
        bwd = jnp.where(lane == x + 64, 1.0 - 0.7 * zsol[1, x][:, 0:1].astype(f32), bwd)
        return fwd, bwd

    zero = jnp.zeros((CY, 128), f32)
    fwd, bwd = lax.fori_loop(0, CX, columns, (zero, zero))
    zfwd[...] = fwd
    zbwd[...] = bwd
    faces.append(send(zfwd, zlo, {"gz": lax.rem(gz + 1, 4)}))
    faces.append(send(zbwd, zhi, {"gz": lax.rem(gz + 3, 4)}))
    keep_z = pltpu.make_async_copy(zbwd, zown, osem.at[2])
    keep_z.start()

    for copy in second:
        copy.wait_recv()
    third = [
        send(rall.at[:, core, gy], rall.at[:, core, gy], {"gy": lax.rem(gy + o, 8)})
        for o in range(1, 8)
    ]
    for copy in third:
        copy.wait_recv()
    last = send(rall.at[:, core], rall.at[:, core], {"gx": gx + 1 - 2 * core})
    last.wait_recv()
    for copy in faces:
        copy.wait_recv()
    for copy in started:
        copy.wait_send()
    keep_y.wait()
    keep_z.wait()


def call_faces(conc, adj, vx, vy, vz, solid, rates):
    face = lambda *s: jax.ShapeDtypeStruct(s, f32)
    outs = (
        face(3, CY, CZ), jax.ShapeDtypeStruct((CY, CZ), i32),
        face(2, CY, CZ), jax.ShapeDtypeStruct((CY, CZ), i32),
        face(4, CX, CZ), face(3, CX, CZ),
        face(CY, 128), face(CY, 128), face(3, CX, CZ), face(CY, 128),
        face(2, 2, 8, 4, 16, 128),
    )
    return pl.pallas_call(
        gather_faces,
        out_shape=outs,
        in_specs=[ANY] * 7,
        out_specs=[ANY] * len(outs),
        scratch_shapes=[
            pltpu.VMEM((5, CX, 8, CZ), f32), pltpu.VMEM((2, CX, 8, CZ), i32),
            pltpu.VMEM((5, CX, CY, 128), f32), pltpu.VMEM((2, CX, CY, 128), i32),
            pltpu.VMEM((4, CX, CZ), f32), pltpu.VMEM((3, CX, CZ), f32),
            pltpu.VMEM((CY, 128), f32), pltpu.VMEM((CY, 128), f32),
            pltpu.SemaphoreType.DMA((14,)), pltpu.SemaphoreType.DMA((24,)),
            pltpu.SemaphoreType.DMA((3,)), pltpu.SemaphoreType.DMA((24,)),
            pltpu.SemaphoreType.DMA((1,)),
        ],
        compiler_params=pltpu.CompilerParams(
            collective_id=0, has_side_effects=True, vmem_limit_bytes=40 << 20
        ),
    )(conc, adj, vx, vy, vz, solid, rates)


def roll_tile(tile, shift):
    return pltpu.roll(tile, shift, 1)


def main_kernel(
    block_ref,
    conc_ref, conc_next, adj_ref, adj_next, solid_ref, solid_next, load_ref, adjload_ref,
    vx_ref, vy_ref, vz_ref, slot_ref,
    xlo, xlo_s, xhi, xhi_s, ylo, yhi, zlo, zhi, yown, zown, rall, home0, home1, slot_grain,
    fin_ref, mstart_ref, dense_ref, lx_ref, ly_ref, lz_ref, cx_ref, cy_ref, cz_ref,
    packed, places_ref, table, hx, qx, hy, qy, hz, gp, lp, bxp, axp, qpp,
    hi_f, lo_f, term_f, hot_lo, hot_hi, total,
):
    i = pl.program_id(0)
    gx, gy, gz = (lax.axis_index(a) for a in ("gx", "gy", "gz"))
    has = lambda cond: jnp.where(cond, 1.0, 0.0).astype(f32)
    lo_x, hi_x = has(gx > 0), has(gx < 3)
    lo_y, hi_y = has(gy > 0), has(gy < 7)
    lo_z, hi_z = has(gz > 0), has(gz < 3)
    lane1 = lax.broadcasted_iota(i32, (CY, 128), 1)
    weight_of = lambda s: 1.0 - 0.7 * s.astype(f32)

    def pair(w0, w1, v):
        k = (dispersion * w0) * w1
        return k - jnp.minimum(v, 0.0), k + jnp.maximum(v, 0.0)

    @pl.when(i == 0)
    def _():
        total[...] = jnp.zeros_like(total)
        def pack(r, carry):
            at = pl.ds(pl.multiple_of(r * 64, 64), 64)
            up = pl.ds(pl.multiple_of(r * 64 + 1024, 64), 64)
            low = (rall[at, :] * (1.0 / rate_step) + 0.5).astype(i32)
            high = (rall[up, :] * (1.0 / rate_step) + 0.5).astype(i32)
            packed[at, :] = low + (high << 16)
            return carry

        lax.fori_loop(0, 16, pack, 0)
        base = (slot_grain[...] - block_ref[0] * 2048) & 262143
        lanes = [base[8 * j:8 * j + 8] & 127 for j in range(4)]
        rows = [base[8 * j:8 * j + 8] >> 7 for j in range(4)]
        found = [jnp.zeros((8, 128), i32)] * 4
        for r in range(32):
            src = home0 if r < 16 else home1
            row = jnp.broadcast_to(src[0, r % 16:r % 16 + 1, :], (8, 128))
            for j in range(4):
                found[j] = jnp.where(
                    rows[j] == r, jnp.take_along_axis(row, lanes[j], axis=1), found[j]
                )
        for j in range(4):
            places_ref[8 * j:8 * j + 8, :] = found[j]
        lanes = [f & 127 for f in found]
        rows = [(f >> 7) & 1023 for f in found]

        def look(r8, acc):
            acc = list(acc)
            for u in range(8):
                r = r8 * 8 + u
                row = jnp.broadcast_to(packed[pl.ds(r, 1), :], (8, 128))
                for j in range(4):
                    acc[j] = jnp.where(
                        rows[j] == r, jnp.take_along_axis(row, lanes[j], axis=1), acc[j]
                    )
            return tuple(acc)

        got = lax.fori_loop(0, 128, look, tuple(jnp.zeros((8, 128), i32) for _ in range(4)))
        got = [
            jnp.where(found[j] >= 131072, lax.shift_right_logical(got[j], 16), got[j] & 65535)
            for j in range(4)
        ]
        table[0:8, :] = got[0] + (got[2] << 16)
        table[8:16, :] = got[1] + (got[3] << 16)

        a, b = pair(weight_of(xlo_s[...]) * lo_x, weight_of(solid_ref[0]), xlo[2] * lo_x)
        hx[...] = a * conc_ref[0] - b * (xlo[0] * lo_x)
        qx[...] = a * (adj_ref[0] - xlo[1] * lo_x)
        cx_ref[0] = a
        a, b = pair(ylo[3] * lo_y, yown[2], ylo[2] * lo_y)
        hy[...] = a * yown[0] - b * (ylo[0] * lo_y)
        qy[...] = a * (yown[1] - ylo[1] * lo_y)
        cy_ref[0] = a
        low = zlo[...] * lo_z
        own = zown[...]
        own_w = roll_tile(own, 64)
        a, b = pair(roll_tile(low, 32), own_w, roll_tile(low, 64))
        flux_c = a * own - b * low
        flux_l = a * (roll_tile(own, 96) - roll_tile(low, 96))
        hz[...] = jnp.where(lane1 < 32, flux_c, roll_tile(jnp.where(lane1 < 32, flux_l, 0.0), 32))
        cz_ref[...] = jnp.where(lane1 < 32, a, 0.0)
        lz_ref[...] = jnp.zeros_like(lz_ref)

    ri = lax.broadcasted_iota(i32, (CY, CZ), 0)
    li = lax.broadcasted_iota(i32, (CY, CZ), 1)
    at = pl.ds(i, 1)
    two = lambda tile: jnp.concatenate([tile, tile], axis=1)
    lane_first = lambda tile, k: two(roll_tile(tile, lax.rem(256 - i - 32 * k, 128)))
    lane_last = lambda tile, k: two(roll_tile(tile, lax.rem(255 - i - 32 * k, 128)))

    def up_y(v, row):
        return jnp.where(ri == CY - 1, row, pltpu.roll(v, CY - 1, 0))

    def down_y(v, row):
        return jnp.where(ri == 0, row, pltpu.roll(v, 1, 0))

    def up_z(v, tile):
        return jnp.where(li == CZ - 1, tile, pltpu.roll(v, CZ - 1, 1))

    def down_z(v, tile):
        return jnp.where(li == 0, tile, pltpu.roll(v, 1, 1))

    c, l = conc_ref[0], adj_ref[0]
    sol = solid_ref[0].astype(f32)
    w = 1.0 - 0.7 * sol
    end = i == CX - 1
    w1 = jnp.where(end, weight_of(xhi_s[...]) * hi_x, weight_of(solid_next[0]))
    c1 = jnp.where(end, xhi[0] * hi_x, conc_next[0])
    l1 = jnp.where(end, xhi[1] * hi_x, adj_next[0])
    ax, bx = pair(w, w1, vx_ref[0])
    flux = ax * c1 - bx * c
    div = flux - hx[...]
    hx[...] = flux
    d = l1 - l
    q = ax * d
    lap = bx * d - qx[...]
    qx[...] = q
    ay, by = pair(w, up_y(w, yhi[2, at, :] * hi_y), vy_ref[0])
    flux = ay * up_y(c, yhi[0, at, :] * hi_y) - by * c
    div = div + flux - down_y(flux, hy[at, :])
    d = up_y(l, yhi[1, at, :] * hi_y) - l
    q = ay * d
    lap = lap + by * d - down_y(q, qy[at, :])
    high = zhi[...] * hi_z
    az, bz = pair(w, up_z(w, lane_last(high, 2)), vz_ref[0])
    flux = az * up_z(c, lane_last(high, 0)) - bz * c
    div = div + flux - down_z(flux, lane_first(hz[...], 0))
    d = up_z(l, lane_last(high, 1)) - l
    q = az * d
    lap = lap + bz * d - down_z(q, lane_first(hz[...], 1))

    lookups = []
    for g in range(CY // 8):
        halves = []
        for h in range(2):
            s = slot_ref[0, 8 * g:8 * g + 8, 128 * h:128 * h + 128]
            lo, hi = s & 127, s >> 7
            level = [
                jnp.take_along_axis(jnp.broadcast_to(table[r:r + 1, :], (8, 128)), lo, axis=1)
                for r in range(16)
            ]
            for bit in range(4):
                mask = (hi & (1 << bit)) != 0
                level = [
                    jnp.where(mask, level[2 * j + 1], level[2 * j]) for j in range(len(level) // 2)
                ]
            p = level[0]
            value = jnp.where((hi & 16) != 0, lax.shift_right_logical(p, 16), p & 65535)
            halves.append(value.astype(f32) * rate_step)
        lookups.append(jnp.concatenate(halves, axis=1))
    kv = sol * jnp.concatenate(lookups, axis=0)

    def inverse(v):
        r = pl.reciprocal(v, approx=True)
        return r * (2.0 - v * r)

    m = adjload_ref[0]
    u0 = inverse(1.0 + c)
    e0 = c * u0 - load_ref[0]
    r = kv * e0
    conc1 = c + div - r
    load1 = load_ref[0] + r
    d1 = m - l
    u1 = inverse(1.0 + conc1)
    kd = kv * d1
    adj1 = l + lap + kd * (u1 * u1)
    m1 = m - kd
    d0 = m1 - adj1
    kd = kv * d0
    mstart_ref[0] = m1 - kd
    term_f[...] = sol * ((conc1 * u1 - load1) * d1 + e0 * d0)
    base = adj1 + kd * (u0 * u0)

    d = up_y(adj1, 0.0) - adj1
    base = base + by * d - down_y(ay * d, cy_ref[0, at, :] * adj1[0:1, :])
    d = up_z(adj1, 0.0) - adj1
    first_col = lane_first(cz_ref[...], 0) * adj1
    base = base + bz * d - down_z(az * d, first_col)

    @pl.when(i == 0)
    def _():
        qpp[...] = cx_ref[0] * adj1
        lx_ref[0] = adj1

    @pl.when(i > 0)
    def _():
        dx = adj1 - lp[...]
        fin_ref[i - 1] = gp[...] + bxp[...] * dx - qpp[...]
        qpp[...] = axp[...] * dx

    @pl.when(end)
    def _():
        fin_ref[CX - 1] = base - bx * adj1 - qpp[...]
        lx_ref[1] = adj1
        cx_ref[1] = bx

    gp[...] = base
    lp[...] = adj1
    bxp[...] = bx
    axp[...] = ax
    ly_ref[0, at, :] = adj1[0:1, :]
    ly_ref[1, at, :] = adj1[CY - 1:CY, :]
    cy_ref[1, at, :] = by[CY - 1:CY, :]
    packed_l = jnp.where(lane1 == i, adj1[:, 0:1], lz_ref[...])
    lz_ref[...] = jnp.where(lane1 == i + 32, adj1[:, CZ - 1:CZ], packed_l)
    cz_ref[...] = jnp.where(lane1 == i + 32, bz[:, CZ - 1:CZ], cz_ref[...])

    slots = slot_ref[0]
    hi_f[...] = (slots >> 7).astype(f32)
    lo_f[...] = (slots & 127).astype(f32)
    ids = lax.broadcasted_iota(i32, (128, CZ), 0).astype(f32).astype(bf16)
    zero, one = jnp.zeros((16, CZ), bf16), jnp.ones((16, CZ), bf16)
    row = lambda ref, y: jnp.broadcast_to(ref[y:y + 1, :], (16, CZ))
    acc = total[...]
    for chunk in range(8):
        slot = chunk % 4
        for y8 in range(8):
            y = chunk * 8 + y8
            span = slice(y8 * CZ, y8 * CZ + CZ)
            h, o = row(hi_f, y).astype(bf16), row(lo_f, y).astype(bf16)
            t = row(term_f, y)
            t_high = t.astype(bf16)
            t_low = (t - t_high.astype(f32)).astype(bf16)
            for j in range(2):
                mask = ids[16 * j:16 * j + 16] == h
                hot_hi[slot, 16 * j:16 * j + 16, span] = jnp.where(mask, t_high, zero)
                hot_hi[slot, 32 + 16 * j:48 + 16 * j, span] = jnp.where(mask, t_low, zero)
            for j in range(8):
                hot_lo[slot, 16 * j:16 * j + 16, span] = jnp.where(
                    ids[16 * j:16 * j + 16] == o, one, zero
                )
        acc = acc + lax.dot_general(
            hot_lo[slot], hot_hi[slot], (((1,), (1,)), ((), ())), preferred_element_type=f32
        )
    total[...] = acc

    @pl.when(end)
    def _():
        by_lane = total[...].T
        sums = by_lane[0:32] + by_lane[32:64]
        places = places_ref[...]
        high = sums.astype(bf16)
        high_f = high.astype(f32)
        low_f = sums - high_f
        place_lane = (places & 127).astype(f32)
        place_row = places >> 7
        lane_ids = lax.broadcasted_iota(i32, (128, 128), 0).astype(f32)

        row_ids = lax.broadcasted_iota(i32, (256, 128), 0)

        hots = []
        values = []
        for s in range(32):
            match = lane_ids == place_lane[s:s + 1, :]
            values.append(
                jnp.concatenate(
                    [
                        jnp.where(match, high_f[s:s + 1, :], 0.0).astype(bf16),
                        jnp.where(match, low_f[s:s + 1, :], 0.0).astype(bf16),
                    ],
                    axis=0,
                )
            )
        value = jnp.concatenate(values, axis=1)

        def spread(n, carry):
            hot = jnp.concatenate(
                [
                    jnp.where(row_ids + n * 256 == place_row[s:s + 1, :], 1.0, 0.0).astype(bf16)
                    for s in range(32)
                ],
                axis=1,
            )
            got = lax.dot_general(
                hot, value, (((1,), (1,)), ((), ())), preferred_element_type=f32
            )
            dense_ref[pl.ds(pl.multiple_of(n * 256, 256), 256), :] = got[:, 0:128] + got[:, 128:256]
            return carry

        lax.fori_loop(0, 8, spread, 0)


def call_main(block, arrays, faces, home, slot_grain):
    conc, load, adj, adj_load, vx, vy, vz, solid, slot = arrays
    plane = pl.BlockSpec((1, CY, CZ), lambda i, b: (i, 0, 0))
    after = pl.BlockSpec((1, CY, CZ), lambda i, b: (jnp.minimum(i + 1, CX - 1), 0, 0))

    def whole(shape):
        return pl.BlockSpec(shape, lambda i, b: (0,) * len(shape))

    face_shapes = [
        (3, CY, CZ), (CY, CZ), (2, CY, CZ), (CY, CZ), (4, CX, CZ), (3, CX, CZ),
        (CY, 128), (CY, 128), (3, CX, CZ), (CY, 128), (2048, 128),
    ]
    out_shapes = [
        (CX, CY, CZ), (CX, CY, CZ), (2048, 128), (2, CY, CZ), (2, CX, CZ), (CY, 128),
        (2, CY, CZ), (2, CX, CZ), (CY, 128),
    ]
    plane_scratch = pltpu.VMEM((CY, CZ), f32)
    row_scratch = pltpu.VMEM((CX, CZ), f32)
    return pl.pallas_call(
        main_kernel,
        out_shape=[jax.ShapeDtypeStruct(s, f32) for s in out_shapes],
        grid_spec=pltpu.PrefetchScalarGridSpec(
            num_scalar_prefetch=1,
            grid=(CX,),
            in_specs=[plane, after, plane, after, plane, after, plane, plane, plane, plane, plane, plane]
            + [whole(s) for s in face_shapes]
            + [
                pl.BlockSpec((1, 16, 128), lambda i, b: (b[0], 0, 0)),
                pl.BlockSpec((1, 16, 128), lambda i, b: (lax.rem(b[0] + 1, 128), 0, 0)),
                whole((32, 128)),
            ],
            out_specs=[whole(out_shapes[0]), plane] + [whole(s) for s in out_shapes[2:]],
            scratch_shapes=[
                pltpu.VMEM((1024, 128), i32), pltpu.VMEM((32, 128), i32), pltpu.VMEM((16, 128), i32),
                plane_scratch, plane_scratch, row_scratch, row_scratch, pltpu.VMEM((CY, 128), f32),
                plane_scratch, plane_scratch, plane_scratch, plane_scratch, plane_scratch,
                plane_scratch, plane_scratch, plane_scratch,
                pltpu.VMEM((4, 128, 2048), bf16), pltpu.VMEM((4, 64, 2048), bf16),
                pltpu.VMEM((128, 64), f32),
            ],
        ),
        compiler_params=pltpu.CompilerParams(
            dimension_semantics=("arbitrary",), vmem_limit_bytes=50 << 20
        ),
        cost_estimate=pl.CostEstimate(flops=10 ** 9, bytes_accessed=25 << 20, transcendentals=0),
    )(
        block, conc, conc, adj, adj, solid, solid, load, adj_load, vx, vy, vz, slot,
        *faces[:10], faces[10].reshape(2048, 128), home, home, slot_grain,
    )


def finish_kernel(
    fin, dense, lx, ly, lz, cx, cy, cz,
    out, grad,
    fbuf, xlo, xhi, ylo, yhi, zlo, zhi, d1, r1, r2, s2, r3, s3, r4, lsem, ssem, rsem,
):
    gx, gy, gz = (lax.axis_index(a) for a in ("gx", "gy", "gz"))
    xh, core = gx // 2, lax.rem(gx, 2)
    has = lambda cond: jnp.where(cond, 1.0, 0.0).astype(f32)
    hi_x, hi_y, hi_z = has(gx < 3), has(gy < 7), has(gz < 3)
    keep = pltpu.make_async_copy(dense.at[:, core], d1, lsem.at[0])
    keep.start()
    body = pltpu.make_async_copy(fin, fbuf, lsem.at[1])
    body.start()
    greet()
    started = []

    def send(src, dst, where):
        k = len(started)
        copy = pltpu.make_async_remote_copy(
            src_ref=src, dst_ref=dst, send_sem=ssem.at[k], recv_sem=rsem.at[k],
            device_id=where, device_id_type=MESH,
        )
        copy.start()
        started.append(copy)
        return copy

    first = send(dense.at[:, 1 - core], r1, {"gx": gx + 1 - 2 * core})
    faces = [
        send(lx.at[1], xlo, {"gx": lax.rem(gx + 1, 4)}),
        send(lx.at[0], xhi, {"gx": lax.rem(gx + 3, 4)}),
        send(ly.at[1], ylo, {"gy": lax.rem(gy + 1, 8)}),
        send(ly.at[0], yhi, {"gy": lax.rem(gy + 7, 8)}),
        send(lz, zlo, {"gz": lax.rem(gz + 1, 4)}),
        send(lz, zhi, {"gz": lax.rem(gz + 3, 4)}),
    ]
    keep.wait()
    first.wait_recv()

    def add_first(h, carry):
        for x in range(2):
            d1[x, h] = d1[x, h] + r1[x, h]
        return carry

    lax.fori_loop(0, 8, add_first, 0)
    second = [
        send(d1.at[:, lax.rem(gy + o, 8)], r2.at[o - 1], {"gy": lax.rem(gy + o, 8)})
        for o in range(1, 8)
    ]
    body.wait()
    for copy in faces:
        copy.wait_recv()
    fbuf[0] = fbuf[0] + cx[0] * xlo[...]
    fbuf[CX - 1] = fbuf[CX - 1] + cx[1] * (xhi[...] * hi_x)
    lane = lax.broadcasted_iota(i32, (CY, 128), 1)
    cols = cz[...] * jnp.where(
        lane < 32, pltpu.roll(zlo[...], 96, 1), pltpu.roll(zhi[...] * hi_z, 32, 1)
    )

    def fix(x, carry):
        at = pl.ds(x, 1)
        fbuf[x, 0:1, :] = fbuf[x, 0:1, :] + cy[0, at, :] * ylo[at, :]
        fbuf[x, CY - 1:CY, :] = fbuf[x, CY - 1:CY, :] + cy[1, at, :] * (yhi[at, :] * hi_y)
        low = pltpu.roll(cols, lax.rem(128 - x, 128), 1)
        high = pltpu.roll(cols, 95 - x, 1)
        fbuf[x, :, 0:128] = fbuf[x, :, 0:128] + jnp.where(lane == 0, low, 0.0)
        fbuf[x, :, 128:256] = fbuf[x, :, 128:256] + jnp.where(lane == 127, high, 0.0)
        return carry

    lax.fori_loop(0, CX, fix, 0)
    store = pltpu.make_async_copy(fbuf, out, lsem.at[2])
    store.start()
    for copy in second:
        copy.wait_recv()
    for x in range(2):
        acc = d1[x, gy]
        for o in range(7):
            acc = acc + r2[o, x]
        s2[x] = acc
    third = [
        send(s2.at[:, lax.rem(gz + o, 4)], r3.at[o - 1], {"gz": lax.rem(gz + o, 4)})
        for o in range(1, 4)
    ]
    for copy in third:
        copy.wait_recv()
    for x in range(2):
        s3[x] = s2[x, gz] + r3[0, x] + r3[1, x] + r3[2, x]
    last = send(s3.at[1 - xh], r4, {"gx": gx + 2 - 4 * xh})
    last.wait_recv()
    grad[...] = s3[xh] + r4[...]
    for copy in started:
        copy.wait_send()
    store.wait()


def call_finish(fin, dense, lx, ly, lz, cx, cy, cz):
    vmem = pl.BlockSpec(memory_space=pltpu.VMEM)
    return pl.pallas_call(
        finish_kernel,
        out_shape=(
            jax.ShapeDtypeStruct((CX, CY, CZ), f32), jax.ShapeDtypeStruct((16, 128), f32)
        ),
        in_specs=[ANY] * 5 + [vmem] * 3,
        out_specs=(ANY, vmem),
        scratch_shapes=[
            pltpu.VMEM((CX, CY, CZ), f32),
            pltpu.VMEM((CY, CZ), f32), pltpu.VMEM((CY, CZ), f32),
            pltpu.VMEM((CX, CZ), f32), pltpu.VMEM((CX, CZ), f32),
            pltpu.VMEM((CY, 128), f32), pltpu.VMEM((CY, 128), f32),
            pltpu.VMEM((2, 8, 4, 16, 128), f32), pltpu.VMEM((2, 8, 4, 16, 128), f32),
            pltpu.VMEM((7, 2, 4, 16, 128), f32), pltpu.VMEM((2, 4, 16, 128), f32),
            pltpu.VMEM((3, 2, 16, 128), f32), pltpu.VMEM((2, 16, 128), f32),
            pltpu.VMEM((16, 128), f32),
            pltpu.SemaphoreType.DMA((3,)), pltpu.SemaphoreType.DMA((18,)),
            pltpu.SemaphoreType.DMA((18,)),
        ],
        compiler_params=pltpu.CompilerParams(
            collective_id=1, has_side_effects=True, vmem_limit_bytes=40 << 20
        ),
    )(fin, dense, lx, ly, lz, cx, cy, cz)


def per_device(
    conc, load, adj_conc, adj_load, vel_x, vel_y, vel_z, solid, voxel_slot, slot_grain, grain_home, rates
):
    block = (lax.axis_index("gx") * 32 + lax.axis_index("gy") * 4 + lax.axis_index("gz")).astype(i32)
    faces = call_faces(conc, adj_conc, vel_x, vel_y, vel_z, solid, rates.reshape(16, 128))
    arrays = (conc, load, adj_conc, adj_load, vel_x, vel_y, vel_z, solid, voxel_slot)
    fin, load_start, dense, lx, ly, lz, cx, cy, cz = call_main(
        block.reshape(1), arrays, faces, grain_home.reshape(128, 16, 128), slot_grain.reshape(32, 128)
    )
    start, grad = call_finish(
        fin, dense.reshape(2, 2, 8, 4, 16, 128), lx, ly, lz, cx, cy, cz
    )
    return start, load_start, grad.reshape(2048)


def solution(mesh):
    cells = P("gx", "gy", "gz")
    every = P(("gx", "gy", "gz"))
    return jax.shard_map(
        per_device,
        mesh=mesh,
        in_specs=(cells,) * 9 + (P(("gx", "gy", "gz"), None), P(), every),
        out_specs=(cells, cells, every),
        check_vma=False,
    )
```

time: 1060 us -> 161 us (0.15)
  matrix products: 303 us -> 0 us
  waiting for transfers between devices: 290 us -> 0 us
  local copies, waits for them, and re-layouts: 231 us -> 13.7 us
  other arithmetic: 184 us -> 0 us
  Pallas kernels: 0 us -> 145 us
  starting transfers between devices: 34.9 us -> 0 us
  between operations: 14.5 us -> 0.69 us
    dot_general x16 -> x0, matrix products: 303 us -> none  [the longest x8 166 us: accumulate(): jnp.einsum('nh,nl->hl', upper_hot, lower_hot, precision=lax.Precision.HIG...]
    all_gather x1 -> x0, waiting for transfers between devices: 170 us -> none  [per_device(): rates_all = lax.all_gather(rates, ('gx', 'gy', 'gz'), axis=0, tiled=True)]
    pallas_call x0 -> x3, Pallas kernels: none -> 145 us  [the longest x1 99.1 us: call_main(): pl.pallas_call(main_kernel, out_shape=[jax.ShapeDtypeStruct(s, f32) for s...]
    unnamed x3 -> x0, waiting for transfers between devices: 115 us -> none
    gather x2 -> x0, local copies, waits for them, and re-layouts: 71.5 us -> none  [the longest x1 48.5 us: per_device(): slot_rate = rates_all[places]]
    dynamic_update_slice x8 -> x0, local copies, waits for them, and re-layouts: 48.1 us -> none  [per_device(): lax.scan(lookup, jnp.zeros((), jnp.float32), label_blocks)]
    sub x2 -> x0, other arithmetic: 39.9 us -> none  [the longest x1 34.3 us: forward(): return (centre + dispersion * spread + transport - uptake, load + uptake)]
    ppermute x12 -> x0, starting transfers between devices: 34.9 us -> none  [the longest x6 25.7 us: with_halo(): lax.ppermute(lax.slice_in_dim(block, block.shape[dim] - width, None, axis...]
  transfers between devices with their start and end apart: 14 -> 0, of which waited for: 4 -> 0; matrix products, arithmetic and copies ran while one was open for 38% -> 0% of each run, Pallas kernels for 0% -> 0%
where the time goes in v1:
time: 161 us; the launch traced here: 159 us
  Pallas kernels  145 us (90%)
  local copies, waits for them, and re-layouts  13.7 us (9%)
    pallas_call x1, Pallas kernels, call_main(): pl.pallas_call(main_kernel, out_shape=[jax.ShapeDtypeStruct(s, f32) for s...  99.1 us
    pallas_call x1, Pallas kernels, call_faces(): pl.pallas_call(gather_faces, out_shape=outs, in_specs=[ANY] * 7, out_spec...  26.2 us
    pallas_call x1, Pallas kernels, call_finish(): pl.pallas_call(finish_kernel, out_shape=(jax.ShapeDtypeStruct((CX, CY, CZ...  19.5 us
    unnamed x20, local copies, waits for them, and re-layouts  13.7 us

profile of v1, /device:TPU:1, one launch (start us, length us, event | category | flops | bytes accessed | tf_op | source)
XLA Modules:
  0.0 159.2 jit_solution(8023692800085170382)
XLA Ops:
  0.6 0.0 copy-start
  0.7 1.6 copy-done
  2.2 0.0 copy-start.1
  2.2 1.6 copy-done.1
  3.8 0.0 copy-start.2
  3.8 1.6 copy-done.2
  5.4 0.0 copy-start.3
  5.4 1.6 copy-done.3
  7.0 0.0 copy-start.4
  7.0 1.6 copy-done.4
  8.6 0.0 copy-start.5
  8.6 1.6 copy-done.5
  10.2 0.0 copy-start.8
  10.2 0.7 copy-done.8
  10.9 0.0 copy-start.7
  10.9 26.2 %shard_map.139 = (f32[3,64,256]{2,1,0:T(8,128)S(1)}, s32[64,256]{1,0:T(8,128)S(1)}, f32[2,64,256]{2,1,0:T(8,128)S(1)}, s32[64,256]{1,0:T(8,128)S(1)}, f32[4,32,2...) custom-call(f32[32,64,256]{2,1,0:T(8,128)S(1)} %copy-done, ...), custom_call_target="tpu_custom_call" | custom-call | tf_op jit(solution)/shard_map/pallas_call | solution.py:151
  37.1 0.0 copy-done.7
  37.1 99.1 %shard_map.140 = (f32[32,64,256]{2,1,0:T(8,128)}, f32[32,64,256]{2,1,0:T(8,128)}, f32[2048,128]{1,0:T(8,128)S(1)}, f32[2,64,256]{2,1,0:T(8,128)S(1)}, f32[2,32,2...) custom-call(s32[1]{0:T(128)} %bitcast.block_ref, ...), custom_call_target="tpu_custom_call" | custom-call | flops 1000000000 | bytes 26214400 | tf_op jit(solution)/shard_map/pallas_call | solution.py:479
  136.2 0.0 copy-start.6
  136.2 1.6 copy-done.6
  137.8 19.5 %shard_map.141 = (f32[32,64,256]{2,1,0:T(8,128)S(1)}, f32[16,128]{1,0:T(8,128)S(1)}) custom-call(f32[32,64,256]{2,1,0:T(8,128)S(1)} %copy-done.6, f32[2,2,8,4,16,128]{5,4,3,2,1,0:T(8,128)S(1)} %bitcast.7, f32[2,64,256]{2,1,0:T(8,128)S(1)} %get-tuple-element.38.lx, f32[2,32,256]{2,1,0:T(8,128)S(1)} %get-tuple-element.39.ly, ...), custom_call_target="tpu_custom_call" | custom-call | tf_op jit(solution)/shard_map/pallas_call | solution.py:608
  157.3 1.3 copy.17
  158.6 0.6 copy.18
Async XLA Ops:
  0.6 1.6 %copy-start = (f32[32,64,256]{2,1,0:T(8,128)S(1)}, f32[32,64,256]{2,1,0:T(8,128)}, u32[]{:S(2)}) copy-start(f32[32,64,256]{2,1,0:T(8,128)} %conc_next.1) | copy-start | bytes 6291460
  2.2 1.6 copy-start.1
  3.8 1.6 copy-start.2
  5.4 1.6 copy-start.3
  7.0 1.6 copy-start.4
  8.6 1.6 copy-start.5
  10.2 0.7 copy-start.8
  10.9 26.2 %copy-start.7 = (s32[1,4096]{1,0:T(1,128)S(1)}, s32[1,4096]{1,0:T(1,128)}, u32[]{:S(2)}) copy-start(s32[1,4096]{1,0:T(1,128)} %param.21) | copy-start | bytes 49156
  136.2 1.6 %copy-start.6 = (f32[32,64,256]{2,1,0:T(8,128)S(1)}, f32[32,64,256]{2,1,0:T(8,128)}, u32[]{:S(2)}) copy-start(f32[32,64,256]{2,1,0:T(8,128)} %get-tuple-element.36.fin) | copy-start | bytes 6291460

commit v2 on v1

--- a/solution.py
+++ b/solution.py
@@ -7,7 +7,9 @@
 from jax.experimental.pallas import tpu as pltpu
 from jax.sharding import PartitionSpec as P
 
-f32, bf16, i32 = jnp.float32, jnp.bfloat16, jnp.int32
+f32, bf16, i32, f8 = jnp.float32, jnp.bfloat16, jnp.int32, jnp.float8_e4m3fn
+DIGITS = 4
+CHUNKS = 4
 MESH = pl.DeviceIdType.MESH
 ANY = pl.BlockSpec(memory_space=pl.ANY)
 dispersion = 0.06
@@ -163,7 +165,7 @@
             pltpu.SemaphoreType.DMA((1,)),
         ],
         compiler_params=pltpu.CompilerParams(
-            collective_id=0, has_side_effects=True, vmem_limit_bytes=40 << 20
+            collective_id=0, has_side_effects=True, vmem_limit_bytes=62 << 20
         ),
     )(conc, adj, vx, vy, vz, solid, rates)
 
@@ -179,7 +181,7 @@
     xlo, xlo_s, xhi, xhi_s, ylo, yhi, zlo, zhi, yown, zown, rall, home0, home1, slot_grain,
     fin_ref, mstart_ref, dense_ref, lx_ref, ly_ref, lz_ref, cx_ref, cy_ref, cz_ref,
     packed, places_ref, table, hx, qx, hy, qy, hz, gp, lp, bxp, axp, qpp,
-    hi_f, lo_f, term_f, hot_lo, hot_hi, total,
+    hi_f, lo_f, term_f, hot_lo, hot_hi, total, got_ref, look_ref
 ):
     i = pl.program_id(0)
     gx, gy, gz = (lax.axis_index(a) for a in ("gx", "gy", "gz"))
@@ -197,12 +199,11 @@
     @pl.when(i == 0)
     def _():
         total[...] = jnp.zeros_like(total)
+        hot_lo[...] = jnp.zeros_like(hot_lo)
+        hot_hi[...] = jnp.zeros_like(hot_hi)
         def pack(r, carry):
-            at = pl.ds(pl.multiple_of(r * 64, 64), 64)
-            up = pl.ds(pl.multiple_of(r * 64 + 1024, 64), 64)
-            low = (rall[at, :] * (1.0 / rate_step) + 0.5).astype(i32)
-            high = (rall[up, :] * (1.0 / rate_step) + 0.5).astype(i32)
-            packed[at, :] = low + (high << 16)
+            at = pl.ds(pl.multiple_of(r * 128, 128), 128)
+            packed[at, :] = (rall[at, :] * (1.0 / rate_step) + 0.5).astype(i32)
             return carry
 
         lax.fori_loop(0, 16, pack, 0)
@@ -222,22 +223,36 @@
         lanes = [f & 127 for f in found]
         rows = [(f >> 7) & 1023 for f in found]
 
-        def look(r8, acc):
-            acc = list(acc)
-            for u in range(8):
-                r = r8 * 8 + u
-                row = jnp.broadcast_to(packed[pl.ds(r, 1), :], (8, 128))
-                for j in range(4):
-                    acc[j] = jnp.where(
-                        rows[j] == r, jnp.take_along_axis(row, lanes[j], axis=1), acc[j]
+
+        sub_ids = lax.broadcasted_iota(i32, (256, 128), 0).astype(f32).astype(bf16)
+        ones, zeros = jnp.ones((256, 128), bf16), jnp.zeros((256, 128), bf16)
+
+        def look(n, acc):
+            at = pl.ds(pl.multiple_of(n * 256, 256), 256)
+            q = packed[at, :]
+            digits = jnp.concatenate([(q & 255).astype(f32).astype(bf16), ((q >> 8) & 255).astype(f32).astype(bf16)], axis=1)
+            first = (n * 256).astype(f32)
+            hot = jnp.concatenate(
+                [
+                    jnp.where(
+                        sub_ids == jnp.broadcast_to((found[s // 8] >> 7).astype(f32)[s % 8:s % 8 + 1, :] - first, (256, 128)).astype(bf16),
+                        ones, zeros,
                     )
-            return tuple(acc)
-
-        got = lax.fori_loop(0, 128, look, tuple(jnp.zeros((8, 128), i32) for _ in range(4)))
-        got = [
-            jnp.where(found[j] >= 131072, lax.shift_right_logical(got[j], 16), got[j] & 65535)
-            for j in range(4)
-        ]
+                    for s in range(32)
+                ],
+                axis=1,
+            )
+            got_ref[...] = got_ref[...] + lax.dot_general(digits, hot, (((0,), (0,)), ((), ())), preferred_element_type=f32)
+            return acc
+        got_ref[...] = jnp.zeros_like(got_ref)
+        lax.fori_loop(0, 8, look, 0)
+        lids = lax.broadcasted_iota(i32, (128, 128), 0)
+        for s in range(32):
+            m = lids == (found[s // 8] & 127)[s % 8:s % 8 + 1, :]
+            sp = slice(128 * s, 128 * s + 128)
+            v = got_ref[0:128, sp] + 256.0 * got_ref[128:256, sp]
+            look_ref[s:s + 1, :] = jnp.sum(jnp.where(m, v, 0.0), axis=0, keepdims=True)
+        got = [look_ref[8 * j:8 * j + 8, :].astype(i32) for j in range(4)]
         table[0:8, :] = got[0] + (got[2] << 16)
         table[8:16, :] = got[1] + (got[3] << 16)
 
@@ -259,6 +274,17 @@
         cz_ref[...] = jnp.where(lane1 < 32, a, 0.0)
         lz_ref[...] = jnp.zeros_like(lz_ref)
 
+    def products():
+        acc = None
+        for chunk in range(CHUNKS):
+            span = slice(chunk * (CY * CZ // CHUNKS), (chunk + 1) * (CY * CZ // CHUNKS))
+            got = lax.dot_general(
+                hot_lo[:, span], hot_hi[:, span], (((1,), (1,)), ((), ())), preferred_element_type=f32
+            )
+            acc = got if acc is None else acc + got
+        return acc
+
+    total[...] = total[...] + products()
     ri = lax.broadcasted_iota(i32, (CY, CZ), 0)
     li = lax.broadcasted_iota(i32, (CY, CZ), 1)
     at = pl.ds(i, 1)
@@ -387,35 +413,29 @@
     hi_f[...] = (slots >> 7).astype(f32)
     lo_f[...] = (slots & 127).astype(f32)
     ids = lax.broadcasted_iota(i32, (128, CZ), 0).astype(f32).astype(bf16)
-    zero, one = jnp.zeros((16, CZ), bf16), jnp.ones((16, CZ), bf16)
-    row = lambda ref, y: jnp.broadcast_to(ref[y:y + 1, :], (16, CZ))
-    acc = total[...]
-    for chunk in range(8):
-        slot = chunk % 4
-        for y8 in range(8):
-            y = chunk * 8 + y8
-            span = slice(y8 * CZ, y8 * CZ + CZ)
-            h, o = row(hi_f, y).astype(bf16), row(lo_f, y).astype(bf16)
-            t = row(term_f, y)
-            t_high = t.astype(bf16)
-            t_low = (t - t_high.astype(f32)).astype(bf16)
-            for j in range(2):
-                mask = ids[16 * j:16 * j + 16] == h
-                hot_hi[slot, 16 * j:16 * j + 16, span] = jnp.where(mask, t_high, zero)
-                hot_hi[slot, 32 + 16 * j:48 + 16 * j, span] = jnp.where(mask, t_low, zero)
-            for j in range(8):
-                hot_lo[slot, 16 * j:16 * j + 16, span] = jnp.where(
-                    ids[16 * j:16 * j + 16] == o, one, zero
-                )
-        acc = acc + lax.dot_general(
-            hot_lo[slot], hot_hi[slot], (((1,), (1,)), ((), ())), preferred_element_type=f32
-        )
-    total[...] = acc
+    zero, one = jnp.zeros((32, CZ), bf16), jnp.ones((32, CZ), bf16)
+    row = lambda ref, y: jnp.broadcast_to(ref[y:y + 1, :], (32, CZ))
+    for y in range(CY):
+        span = slice(y * CZ, y * CZ + CZ)
+        rest = row(term_f, y)
+        mask = ids[0:32] == row(hi_f, y).astype(bf16)
+        for k in range(DIGITS):
+            digit = rest.astype(f8).astype(f32)
+            hot_hi[32 * k:32 * k + 32, span] = jnp.where(mask, digit.astype(bf16), zero).astype(f8)
+            if k < DIGITS - 1:
+                rest = (rest - digit) * 16.0
+        low = row(lo_f, y).astype(bf16)
+        for j in range(4):
+            at_j = slice(32 * j, 32 * j + 32)
+            hot_lo[at_j, span] = jnp.where(ids[at_j] == low, one, zero).astype(f8)
 
     @pl.when(end)
     def _():
+        total[...] = total[...] + products()
         by_lane = total[...].T
-        sums = by_lane[0:32] + by_lane[32:64]
+        sums = by_lane[32 * DIGITS - 32:32 * DIGITS]
+        for k in range(DIGITS - 2, -1, -1):
+            sums = by_lane[32 * k:32 * k + 32] + sums * (1.0 / 16.0)
         places = places_ref[...]
         high = sums.astype(bf16)
         high_f = high.astype(f32)
@@ -424,9 +444,10 @@
         place_row = places >> 7
         lane_ids = lax.broadcasted_iota(i32, (128, 128), 0).astype(f32)
 
-        row_ids = lax.broadcasted_iota(i32, (256, 128), 0)
-
-        hots = []
+        row_ids = lax.broadcasted_iota(i32, (256, 128), 0).astype(f32).astype(bf16)
+        row_f = place_row.astype(f32)
+        ones, zeros = jnp.ones((256, 128), bf16), jnp.zeros((256, 128), bf16)
+
         values = []
         for s in range(32):
             match = lane_ids == place_lane[s:s + 1, :]
@@ -442,9 +463,13 @@
         value = jnp.concatenate(values, axis=1)
 
         def spread(n, carry):
+            first = (n * 256).astype(f32)
             hot = jnp.concatenate(
                 [
-                    jnp.where(row_ids + n * 256 == place_row[s:s + 1, :], 1.0, 0.0).astype(bf16)
+                    jnp.where(
+                        row_ids == jnp.broadcast_to(row_f[s:s + 1, :] - first, (256, 128)).astype(bf16),
+                        ones, zeros,
+                    )
                     for s in range(32)
                 ],
                 axis=1,
@@ -491,16 +516,16 @@
             ],
             out_specs=[whole(out_shapes[0]), plane] + [whole(s) for s in out_shapes[2:]],
             scratch_shapes=[
-                pltpu.VMEM((1024, 128), i32), pltpu.VMEM((32, 128), i32), pltpu.VMEM((16, 128), i32),
+                pltpu.VMEM((2048, 128), i32), pltpu.VMEM((32, 128), i32), pltpu.VMEM((16, 128), i32),
                 plane_scratch, plane_scratch, row_scratch, row_scratch, pltpu.VMEM((CY, 128), f32),
                 plane_scratch, plane_scratch, plane_scratch, plane_scratch, plane_scratch,
                 plane_scratch, plane_scratch, plane_scratch,
-                pltpu.VMEM((4, 128, 2048), bf16), pltpu.VMEM((4, 64, 2048), bf16),
-                pltpu.VMEM((128, 64), f32),
+                pltpu.VMEM((128, CY * CZ), f8), pltpu.VMEM((32 * DIGITS, CY * CZ), f8),
+                pltpu.VMEM((128, 32 * DIGITS), f32), pltpu.VMEM((256, 4096), f32), pltpu.VMEM((32, 128), f32),
             ],
         ),
         compiler_params=pltpu.CompilerParams(
-            dimension_semantics=("arbitrary",), vmem_limit_bytes=50 << 20
+            dimension_semantics=("arbitrary",), vmem_limit_bytes=58 << 20
         ),
         cost_estimate=pl.CostEstimate(flops=10 ** 9, bytes_accessed=25 << 20, transcendentals=0),
     )(
@@ -625,7 +650,7 @@
             pltpu.SemaphoreType.DMA((18,)),
         ],
         compiler_params=pltpu.CompilerParams(
-            collective_id=1, has_side_effects=True, vmem_limit_bytes=40 << 20
+            collective_id=1, has_side_effects=True, vmem_limit_bytes=62 << 20
         ),
     )(fin, dense, lx, ly, lz, cx, cy, cz)
 

time: 161 us -> 138 us (0.86)
  Pallas kernels: 145 us -> 133 us
  local copies, waits for them, and re-layouts: 13.7 us -> 3.74 us
    pallas_call x1, Pallas kernels: 99.1 us -> 85.6 us  [call_main(): pl.pallas_call(main_kernel, out_shape=[jax.ShapeDtypeStruct(s, f32) for s...]
    unnamed x20 -> x4, local copies, waits for them, and re-layouts: 13.7 us -> 3.74 us
where the time goes in v2:
time: 138 us; the launch traced here: 137 us
  Pallas kernels  133 us (96%)
  local copies, waits for them, and re-layouts  3.74 us (3%)
    pallas_call x1, Pallas kernels, call_main(): pl.pallas_call(main_kernel, out_shape=[jax.ShapeDtypeStruct(s, f32) for s...  85.6 us
    pallas_call x1, Pallas kernels, call_faces(): pl.pallas_call(gather_faces, out_shape=outs, in_specs=[ANY] * 7, out_spec...  26.4 us
    pallas_call x1, Pallas kernels, call_finish(): pl.pallas_call(finish_kernel, out_shape=(jax.ShapeDtypeStruct((CX, CY, CZ...  20.7 us
    unnamed x4, local copies, waits for them, and re-layouts  3.74 us

profile of v2, /device:TPU:1, one launch (start us, length us, event | category | flops | bytes accessed | tf_op | source)
XLA Modules:
  0.0 137.0 jit_solution(13858258017604995621)
XLA Ops:
  0.6 26.4 %shard_map.139 = (f32[3,64,256]{2,1,0:T(8,128)}, s32[64,256]{1,0:T(8,128)}, f32[2,64,256]{2,1,0:T(8,128)}, s32[64,256]{1,0:T(8,128)}, f32[4,32,256]{2,1,0:T(8,12...) custom-call(f32[32,64,256]{2,1,0:T(8,128)} %conc_next.1, ...), custom_call_target="tpu_custom_call" | custom-call | tf_op jit(solution)/shard_map/pallas_call | solution.py:153
  27.0 85.6 %shard_map.140 = (f32[32,64,256]{2,1,0:T(8,128)}, f32[32,64,256]{2,1,0:T(8,128)}, f32[2048,128]{1,0:T(8,128)}, f32[2,64,256]{2,1,0:T(8,128)}, f32[2,32,256]{2,1,...) custom-call(s32[1]{0:T(128)} %bitcast.block_ref, ...), custom_call_target="tpu_custom_call" | custom-call | flops 1000000000 | bytes 26214400 | tf_op jit(solution)/shard_map/pallas_call | solution.py:504
  112.6 20.7 %shard_map.141 = (f32[32,64,256]{2,1,0:T(8,128)}, f32[16,128]{1,0:T(8,128)}) custom-call(f32[32,64,256]{2,1,0:T(8,128)} %get-tuple-element.36.fin, f32[2,2,8,4,16,128]{5,4,3,2,1,0:T(8,128)} %bitcast.9, f32[2,64,256]{2,1,0:T(8,128)} %get-tuple-element.38.lx, f32[2,32,256]{2,1,0:T(8,128)} %get-tuple-element.39.ly, f32[64,128]{1,0:T(8,128)} %get-tuple-element.40.lz, ...), custom_call_target="tpu_custom_call" | custom-call | tf_op jit(solution)/shard_map/pallas_call | solution.py:633
  133.2 0.0 copy-start
  133.2 3.1 %copy.17 = f32[32,64,256]{2,1,0:T(8,128)} copy(f32[32,64,256]{2,1,0:T(8,128)} %get-tuple-element.50) | data formatting | bytes 4194304
  136.4 0.0 copy-done
  136.4 0.6 copy.18
Async XLA Ops:
  133.2 3.1 %copy-start = (f32[16,128]{1,0:T(8,128)S(1)}, f32[16,128]{1,0:T(8,128)}, u32[]{:S(2)}) copy-start(f32[16,128]{1,0:T(8,128)} %get-tuple-element.46) | copy-start | bytes 24580

commit v3 on v2

v3 whole, which is shorter than its diff:
```python
import functools

import jax
import jax.numpy as jnp
from jax import lax
from jax.experimental import pallas as pl
from jax.experimental.pallas import tpu as pltpu
from jax.sharding import PartitionSpec as P

f32, bf16, i32, f8 = jnp.float32, jnp.bfloat16, jnp.int32, jnp.float8_e4m3fn
DIGITS = 3
CHUNKS = 4
MESH = pl.DeviceIdType.MESH
ANY = pl.BlockSpec(memory_space=pl.ANY)
dispersion = 0.06
rate_step = 0.2 / 65535.0
CX, CY, CZ = 32, 64, 256


def greet():
    barrier = pltpu.get_barrier_semaphore()
    for axis, count in (("gx", 4), ("gy", 8), ("gz", 4)):
        me = lax.axis_index(axis)
        for o in range(1, count):
            pl.semaphore_signal(
                barrier, inc=1, device_id={axis: lax.rem(me + o, count)}, device_id_type=MESH
            )
    pl.semaphore_wait(barrier, 13)


def weight_of(s):
    return 1.0 - 0.7 * s.astype(f32)


def pair(w0, w1, v):
    k = (dispersion * w0) * w1
    return k - jnp.minimum(v, 0.0), k + jnp.maximum(v, 0.0)


def plane_iotas():
    return (
        lax.broadcasted_iota(i32, (CY, CZ), 0),
        lax.broadcasted_iota(i32, (CY, CZ), 1),
        lax.broadcasted_iota(i32, (CY, 128), 1),
    )


def shifts(ri, li):
    return (
        lambda v: jnp.where(ri == CY - 1, 0.0, pltpu.roll(v, CY - 1, 0)),
        lambda v: jnp.where(ri == 0, 0.0, pltpu.roll(v, 1, 0)),
        lambda v: jnp.where(li == CZ - 1, 0.0, pltpu.roll(v, CZ - 1, 1)),
        lambda v: jnp.where(li == 0, 0.0, pltpu.roll(v, 1, 1)),
    )


def sender(started, ssem, rsem):
    def send(src, dst, where):
        k = len(started)
        copy = pltpu.make_async_remote_copy(
            src_ref=src, dst_ref=dst, send_sem=ssem.at[k], recv_sem=rsem.at[k],
            device_id=where, device_id_type=MESH,
        )
        copy.start()
        started.append(copy)
        return copy

    return send


def gather_faces(
    conc, adj, vx, vy, vz, solid, rates,
    xlo, xlo_s, xhi, xhi_s, ylo, yhi, zlo, zhi, yown, zown, yend, zend, rall, s1_out, s2_out,
    cb, lb, vxb, vyb, vzb, sb, s1, s2, hx, qx, yfwd, ybwd, zfwd, zbwd, lsem, rsem, osem, ssem,
):
    gx, gy, gz = (lax.axis_index(a) for a in ("gx", "gy", "gz"))
    xh, core = gx // 2, lax.rem(gx, 2)
    local = []
    for q in range(4):
        at = pl.ds(8 * q, 8)
        local.append([
            pltpu.make_async_copy(ref.at[at], buf.at[at], lsem.at[6 * q + k])
            for k, (ref, buf) in enumerate(
                ((conc, cb), (adj, lb), (solid, sb), (vx, vxb), (vy, vyb), (vz, vzb))
            )
        ])
        for copy in local[q]:
            copy.start()
    mine = pltpu.make_async_copy(rates, rall.at[xh, core, gy, gz], osem.at[0])
    mine.start()
    greet()

    started = []
    send = sender(started, ssem, rsem)
    first = send(rates, rall.at[xh, core, gy, gz], {"gx": gx + 2 - 4 * xh})
    right, left = {"gx": lax.rem(gx + 1, 4)}, {"gx": lax.rem(gx + 3, 4)}
    faces = []
    for k, ref in enumerate((conc, adj, vx)):
        faces.append(send(ref.at[CX - 1], xlo.at[k], right))
    faces.append(send(solid.at[CX - 1], xlo_s, right))
    for k, ref in enumerate((conc, adj)):
        faces.append(send(ref.at[0], xhi.at[k], left))
    faces.append(send(solid.at[0], xhi_s, left))

    hx[...] = jnp.zeros_like(hx)
    qx[...] = jnp.zeros_like(qx)
    zfwd[...] = jnp.zeros_like(zfwd)
    zbwd[...] = jnp.zeros_like(zbwd)

    def plane(x, carry):
        ri, li, lane = plane_iotas()
        up_y, down_y, up_z, down_z = shifts(ri, li)
        at = pl.ds(x, 1)
        nx = jnp.minimum(x + 1, CX - 1)
        inside = jnp.where(x < CX - 1, 1.0, 0.0).astype(f32)
        c, l, w = cb[x], lb[x], weight_of(sb[x])
        v_x, v_y, v_z = vxb[x], vyb[x], vzb[x]
        a, b = pair(w, weight_of(sb[nx]) * inside, v_x)
        flux = a * (cb[nx] * inside) - b * c
        div = c + flux - hx[...]
        hx[...] = flux
        d = lb[nx] * inside - l
        lap = l + b * d - qx[...]
        qx[...] = a * d
        a, b = pair(w, up_y(w), v_y)
        flux = a * up_y(c) - b * c
        div = div + flux - down_y(flux)
        d = up_y(l) - l
        lap = lap + b * d - down_y(a * d)
        a, b = pair(w, up_z(w), v_z)
        flux = a * up_z(c) - b * c
        s1[x] = div + flux - down_z(flux)
        d = up_z(l) - l
        s2[x] = lap + b * d - down_z(a * d)
        for k, v in enumerate((c, l, v_y, w)):
            yfwd[k, at, :] = v[CY - 1:CY, :]
        for k, v in enumerate((c, l, w)):
            ybwd[k, at, :] = v[0:1, :]
        pack = zfwd[...]
        for k, v in enumerate((c, l, v_z, w)):
            pack = jnp.where(lane == x + 32 * k, v[:, CZ - 1:CZ], pack)
        zfwd[...] = pack
        pack = zbwd[...]
        for k, v in enumerate((c, l, w)):
            pack = jnp.where(lane == x + 32 * k, v[:, 0:1], pack)
        zbwd[...] = pack
        return carry

    def arrived(q):
        for copy in local[q]:
            copy.wait()

    mine.wait()
    first.wait_recv()
    second = [
        send(rall.at[:, core, gy, gz], rall.at[:, core, gy, gz], {"gz": lax.rem(gz + o, 4)})
        for o in range(1, 4)
    ]
    arrived(0)
    arrived(1)
    lax.fori_loop(0, 5, plane, 0)
    for copy in second:
        copy.wait_recv()
    third = [
        send(rall.at[:, core, gy], rall.at[:, core, gy], {"gy": lax.rem(gy + o, 8)})
        for o in range(1, 8)
    ]
    arrived(2)
    arrived(3)
    lax.fori_loop(5, 24, plane, 0)
    for copy in third:
        copy.wait_recv()
    last = send(rall.at[:, core], rall.at[:, core], {"gx": gx + 1 - 2 * core})
    outs = [
        pltpu.make_async_copy(s1.at[0:24], s1_out.at[0:24], osem.at[1]),
        pltpu.make_async_copy(s2.at[0:24], s2_out.at[0:24], osem.at[2]),
    ]
    for copy in outs:
        copy.start()
    lax.fori_loop(24, CX, plane, 0)
    faces.append(send(yfwd, ylo, {"gy": lax.rem(gy + 1, 8)}))
    faces.append(send(ybwd, yhi, {"gy": lax.rem(gy + 7, 8)}))
    faces.append(send(zfwd, zlo, {"gz": lax.rem(gz + 1, 4)}))
    faces.append(send(zbwd, zhi, {"gz": lax.rem(gz + 3, 4)}))
    keep = [
        pltpu.make_async_copy(s1.at[24:32], s1_out.at[24:32], osem.at[3]),
        pltpu.make_async_copy(s2.at[24:32], s2_out.at[24:32], osem.at[4]),
        pltpu.make_async_copy(yfwd, yend, osem.at[5]),
        pltpu.make_async_copy(ybwd, yown, osem.at[6]),
        pltpu.make_async_copy(zfwd, zend, osem.at[7]),
        pltpu.make_async_copy(zbwd, zown, osem.at[8]),
    ]
    for copy in keep:
        copy.start()
    last.wait_recv()
    for copy in faces:
        copy.wait_recv()
    for copy in started:
        copy.wait_send()
    for copy in outs + keep:
        copy.wait()


def call_faces(conc, adj, vx, vy, vz, solid, rates):
    face = lambda *s: jax.ShapeDtypeStruct(s, f32)
    outs = (
        face(3, CY, CZ), jax.ShapeDtypeStruct((CY, CZ), i32),
        face(2, CY, CZ), jax.ShapeDtypeStruct((CY, CZ), i32),
        face(4, CX, CZ), face(3, CX, CZ),
        face(CY, 128), face(CY, 128), face(3, CX, CZ), face(CY, 128),
        face(4, CX, CZ), face(CY, 128),
        face(2, 2, 8, 4, 16, 128), face(CX, CY, CZ), face(CX, CY, CZ),
    )
    whole = pltpu.VMEM((CX, CY, CZ), f32)
    return pl.pallas_call(
        gather_faces,
        out_shape=outs,
        in_specs=[ANY] * 7,
        out_specs=[ANY] * len(outs),
        scratch_shapes=[
            whole, whole, whole, whole, whole, pltpu.VMEM((CX, CY, CZ), i32), whole, whole,
            pltpu.VMEM((CY, CZ), f32), pltpu.VMEM((CY, CZ), f32),
            pltpu.VMEM((4, CX, CZ), f32), pltpu.VMEM((3, CX, CZ), f32),
            pltpu.VMEM((CY, 128), f32), pltpu.VMEM((CY, 128), f32),
            pltpu.SemaphoreType.DMA((24,)), pltpu.SemaphoreType.DMA((23,)),
            pltpu.SemaphoreType.DMA((9,)), pltpu.SemaphoreType.DMA((23,)),
        ],
        compiler_params=pltpu.CompilerParams(
            collective_id=0, has_side_effects=True, vmem_limit_bytes=62 << 20
        ),
    )(conc, adj, vx, vy, vz, solid, rates)


def roll_tile(tile, shift):
    return pltpu.roll(tile, shift, 1)


def main_kernel(
    block_ref,
    s1_ref, s2_ref, conc_ref, adj_ref, solid_ref, load_ref, adjload_ref, slot_ref, vend_ref,
    xlo, xlo_s, xhi, xhi_s, ylo, yhi, zlo, zhi, yown, zown, yend, zend, rall, home0, home1, slot_grain,
    adj1_ref, base_ref, mstart_ref, dense_ref, ly_ref, lz_ref, cx_ref, cy_ref, cz_ref,
    packed, places_ref, table, xc, yc, zc,
    hi_f, lo_f, term_f, hot_lo, hot_hi, total, got_ref, look_ref,
):
    i = pl.program_id(0)
    gx, gy, gz = (lax.axis_index(a) for a in ("gx", "gy", "gz"))
    has = lambda cond: jnp.where(cond, 1.0, 0.0).astype(f32)
    lo_x, hi_x = has(gx > 0), has(gx < 3)
    lo_y, hi_y = has(gy > 0), has(gy < 7)
    lo_z, hi_z = has(gz > 0), has(gz < 3)
    lane1 = lax.broadcasted_iota(i32, (CY, 128), 1)
    @pl.when(i == 0)
    def _():
        total[...] = jnp.zeros_like(total)
        hot_lo[...] = jnp.zeros_like(hot_lo)
        hot_hi[...] = jnp.zeros_like(hot_hi)
        def pack(r, carry):
            at = pl.ds(pl.multiple_of(r * 128, 128), 128)
            packed[at, :] = (rall[at, :] * (1.0 / rate_step) + 0.5).astype(i32)
            return carry

        lax.fori_loop(0, 16, pack, 0)
        base = (slot_grain[...] - block_ref[0] * 2048) & 262143
        lanes = [base[8 * j:8 * j + 8] & 127 for j in range(4)]
        rows = [base[8 * j:8 * j + 8] >> 7 for j in range(4)]
        found = [jnp.zeros((8, 128), i32)] * 4
        for r in range(32):
            src = home0 if r < 16 else home1
            row = jnp.broadcast_to(src[0, r % 16:r % 16 + 1, :], (8, 128))
            for j in range(4):
                found[j] = jnp.where(
                    rows[j] == r, jnp.take_along_axis(row, lanes[j], axis=1), found[j]
                )
        for j in range(4):
            places_ref[8 * j:8 * j + 8, :] = found[j]
        lanes = [f & 127 for f in found]
        rows = [(f >> 7) & 1023 for f in found]


        sub_ids = lax.broadcasted_iota(i32, (256, 128), 0).astype(f32).astype(bf16)
        ones, zeros = jnp.ones((256, 128), bf16), jnp.zeros((256, 128), bf16)

        def look(n, acc):
            at = pl.ds(pl.multiple_of(n * 256, 256), 256)
            q = packed[at, :]
            digits = jnp.concatenate([(q & 255).astype(f32).astype(bf16), ((q >> 8) & 255).astype(f32).astype(bf16)], axis=1)
            first = (n * 256).astype(f32)
            hot = jnp.concatenate(
                [
                    jnp.where(
                        sub_ids == jnp.broadcast_to((found[s // 8] >> 7).astype(f32)[s % 8:s % 8 + 1, :] - first, (256, 128)).astype(bf16),
                        ones, zeros,
                    )
                    for s in range(32)
                ],
                axis=1,
            )
            got_ref[...] = got_ref[...] + lax.dot_general(digits, hot, (((0,), (0,)), ((), ())), preferred_element_type=f32)
            return acc
        got_ref[...] = jnp.zeros_like(got_ref)
        lax.fori_loop(0, 8, look, 0)
        lids = lax.broadcasted_iota(i32, (128, 128), 0)
        for s in range(32):
            m = lids == (found[s // 8] & 127)[s % 8:s % 8 + 1, :]
            sp = slice(128 * s, 128 * s + 128)
            v = got_ref[0:128, sp] + 256.0 * got_ref[128:256, sp]
            look_ref[s:s + 1, :] = jnp.sum(jnp.where(m, v, 0.0), axis=0, keepdims=True)
        got = [look_ref[8 * j:8 * j + 8, :].astype(i32) for j in range(4)]
        table[0:8, :] = got[0] + (got[2] << 16)
        table[8:16, :] = got[1] + (got[3] << 16)

        a, b = pair(weight_of(xlo_s[...]) * lo_x, weight_of(solid_ref[0]), xlo[2] * lo_x)
        xc[0] = b * (xlo[0] * lo_x) - a * conc_ref[0]
        xc[1] = a * (xlo[1] * lo_x - adj_ref[0])
        cx_ref[0] = a
        a, b = pair(ylo[3] * lo_y, yown[2], ylo[2] * lo_y)
        yc[0] = b * (ylo[0] * lo_y) - a * yown[0]
        yc[1] = a * (ylo[1] * lo_y - yown[1])
        cy_ref[0] = a
        k = (dispersion * yend[3]) * (yhi[2] * hi_y)
        a, b = k - jnp.minimum(yend[2], 0.0), k + jnp.maximum(yend[2], 0.0)
        yc[2] = a * (yhi[0] * hi_y) - k * yend[0]
        yc[3] = b * (yhi[1] * hi_y) - k * yend[1]
        cy_ref[1] = b
        cy_ref[2] = k
        low, own = zlo[...] * lo_z, zown[...]
        a, b = pair(roll_tile(low, 32), roll_tile(own, 64), roll_tile(low, 64))
        low_c = b * low - a * own
        low_l = a * (roll_tile(low, 96) - roll_tile(own, 96))
        coef = jnp.where(lane1 < 32, a, 0.0)
        high, own = zhi[...] * hi_z, zend[...]
        k = (dispersion * roll_tile(own, 32)) * roll_tile(high, 64)
        v = roll_tile(own, 64)
        a, b = k - jnp.minimum(v, 0.0), k + jnp.maximum(v, 0.0)
        high_c = a * high - k * own
        high_l = b * roll_tile(high, 96) - k * roll_tile(own, 96)

        def lay(parts):
            out = parts[0]
            for n in range(1, 4):
                out = jnp.where(lane1 >= 32 * n, roll_tile(parts[n], 32 * n), out)
            return out

        zc[...] = lay([low_c, low_l, high_c, high_l])
        cz_ref[...] = lay([coef, b, k, jnp.zeros_like(k)])
        lz_ref[...] = jnp.zeros_like(lz_ref)

    @pl.when(i == CX - 1)
    def _():
        k = (dispersion * weight_of(solid_ref[0])) * (weight_of(xhi_s[...]) * hi_x)
        v = vend_ref[0]
        a, b = k - jnp.minimum(v, 0.0), k + jnp.maximum(v, 0.0)
        xc[0] = a * (xhi[0] * hi_x) - k * conc_ref[0]
        xc[1] = b * (xhi[1] * hi_x) - k * adj_ref[0]
        cx_ref[1] = b
        cx_ref[2] = k

    def products():
        acc = None
        for chunk in range(CHUNKS):
            span = slice(chunk * (CY * CZ // CHUNKS), (chunk + 1) * (CY * CZ // CHUNKS))
            got = lax.dot_general(
                hot_lo[:, span], hot_hi[:, span], (((1,), (1,)), ((), ())), preferred_element_type=f32
            )
            acc = got if acc is None else acc + got
        return acc

    total[...] = total[...] + products()
    at = pl.ds(i, 1)
    end = i == CX - 1
    ri = lax.broadcasted_iota(i32, (8, CZ), 0)
    edge = jnp.where((i == 0) | end, 1.0, 0.0).astype(f32)

    def with_faces(v, n):
        v = v + edge * xc[n]
        low = roll_tile(zc[...], lax.rem(256 - i - 32 * n, 128))
        high = roll_tile(zc[...], lax.rem(319 - i - 32 * n, 128))
        v = v + jnp.concatenate(
            [jnp.where(lane1 == 0, low, 0.0), jnp.where(lane1 == 127, high, 0.0)], axis=1
        )
        first = v[0:8, :] + jnp.where(ri == 0, yc[n, at, :], 0.0)
        final = v[CY - 8:CY, :] + jnp.where(ri == 7, yc[2 + n, at, :], 0.0)
        return jnp.concatenate([first, v[8:CY - 8, :], final], axis=0)

    c, l = conc_ref[0], adj_ref[0]
    sol = solid_ref[0].astype(f32)

    lookups = []
    for g in range(CY // 8):
        halves = []
        for h in range(2):
            s = slot_ref[0, 8 * g:8 * g + 8, 128 * h:128 * h + 128]
            lo, hi = s & 127, s >> 7
            level = [
                jnp.take_along_axis(jnp.broadcast_to(table[r:r + 1, :], (8, 128)), lo, axis=1)
                for r in range(16)
            ]
            for bit in range(4):
                mask = (hi & (1 << bit)) != 0
                level = [
                    jnp.where(mask, level[2 * j + 1], level[2 * j]) for j in range(len(level) // 2)
                ]
            p = level[0]
            value = jnp.where((hi & 16) != 0, lax.shift_right_logical(p, 16), p & 65535)
            halves.append(value.astype(f32) * rate_step)
        lookups.append(jnp.concatenate(halves, axis=1))
    kv = sol * jnp.concatenate(lookups, axis=0)

    def inverse(v):
        r = pl.reciprocal(v, approx=True)
        return r * (2.0 - v * r)

    m = adjload_ref[0]
    u0 = inverse(1.0 + c)
    e0 = c * u0 - load_ref[0]
    r = kv * e0
    conc1 = with_faces(s1_ref[0], 0) - r
    load1 = load_ref[0] + r
    d1 = m - l
    u1 = inverse(1.0 + conc1)
    kd = kv * d1
    adj1 = with_faces(s2_ref[0], 1) + kd * (u1 * u1)
    m1 = m - kd
    d0 = m1 - adj1
    kd = kv * d0
    mstart_ref[0] = m1 - kd
    term_f[...] = sol * ((conc1 * u1 - load1) * d1 + e0 * d0)
    base_ref[0] = adj1 + kd * (u0 * u0)
    adj1_ref[0] = adj1
    ly_ref[0, at, :] = adj1[0:1, :]
    ly_ref[1, at, :] = adj1[CY - 1:CY, :]
    packed_l = jnp.where(lane1 == i, adj1[:, 0:1], lz_ref[...])
    lz_ref[...] = jnp.where(lane1 == i + 32, adj1[:, CZ - 1:CZ], packed_l)

    slots = slot_ref[0]
    hi_f[...] = (slots >> 7).astype(f32)
    lo_f[...] = (slots & 127).astype(f32)
    ids = lax.broadcasted_iota(i32, (128, CZ), 0).astype(f32).astype(bf16)
    zero, one = jnp.zeros((32, CZ), bf16), jnp.ones((32, CZ), bf16)
    row = lambda ref, y: jnp.broadcast_to(ref[y:y + 1, :], (32, CZ))
    for y in range(CY):
        span = slice(y * CZ, y * CZ + CZ)
        rest = row(term_f, y)
        mask = ids[0:32] == row(hi_f, y).astype(bf16)
        for k in range(DIGITS):
            digit = rest.astype(f8).astype(f32)
            hot_hi[32 * k:32 * k + 32, span] = jnp.where(mask, digit.astype(bf16), zero).astype(f8)
            if k < DIGITS - 1:
                rest = (rest - digit) * 16.0
        low = row(lo_f, y).astype(bf16)
        for j in range(4):
            at_j = slice(32 * j, 32 * j + 32)
            hot_lo[at_j, span] = jnp.where(ids[at_j] == low, one, zero).astype(f8)

    @pl.when(end)
    def _():
        total[...] = total[...] + products()
        by_lane = total[...].T
        sums = by_lane[32 * DIGITS - 32:32 * DIGITS]
        for k in range(DIGITS - 2, -1, -1):
            sums = by_lane[32 * k:32 * k + 32] + sums * (1.0 / 16.0)
        places = places_ref[...]
        high = sums.astype(bf16)
        high_f = high.astype(f32)
        low_f = sums - high_f
        place_lane = (places & 127).astype(f32)
        place_row = places >> 7
        lane_ids = lax.broadcasted_iota(i32, (128, 128), 0).astype(f32)

        row_ids = lax.broadcasted_iota(i32, (256, 128), 0).astype(f32).astype(bf16)
        row_f = place_row.astype(f32)
        ones, zeros = jnp.ones((256, 128), bf16), jnp.zeros((256, 128), bf16)

        values = []
        for s in range(32):
            match = lane_ids == place_lane[s:s + 1, :]
            values.append(
                jnp.concatenate(
                    [
                        jnp.where(match, high_f[s:s + 1, :], 0.0).astype(bf16),
                        jnp.where(match, low_f[s:s + 1, :], 0.0).astype(bf16),
                    ],
                    axis=0,
                )
            )
        value = jnp.concatenate(values, axis=1)

        def spread(n, carry):
            first = (n * 256).astype(f32)
            hot = jnp.concatenate(
                [
                    jnp.where(
                        row_ids == jnp.broadcast_to(row_f[s:s + 1, :] - first, (256, 128)).astype(bf16),
                        ones, zeros,
                    )
                    for s in range(32)
                ],
                axis=1,
            )
            got = lax.dot_general(
                hot, value, (((1,), (1,)), ((), ())), preferred_element_type=f32
            )
            dense_ref[pl.ds(pl.multiple_of(n * 256, 256), 256), :] = got[:, 0:128] + got[:, 128:256]
            return carry

        lax.fori_loop(0, 8, spread, 0)


def call_main(block, arrays, faces, home, slot_grain):
    conc, load, adj, adj_load, vx, solid, slot = arrays
    plane = pl.BlockSpec((1, CY, CZ), lambda i, b: (i, 0, 0))

    def whole(shape):
        return pl.BlockSpec(shape, lambda i, b: (0,) * len(shape))

    face_shapes = [
        (3, CY, CZ), (CY, CZ), (2, CY, CZ), (CY, CZ), (4, CX, CZ), (3, CX, CZ),
        (CY, 128), (CY, 128), (3, CX, CZ), (CY, 128), (4, CX, CZ), (CY, 128), (2048, 128),
    ]
    block_shape = (CX, CY, CZ)
    out_shapes = [
        block_shape, block_shape, block_shape, (2048, 128), (2, CX, CZ), (CY, 128),
        (3, CY, CZ), (3, CX, CZ), (CY, 128),
    ]
    plane_scratch = pltpu.VMEM((CY, CZ), f32)
    return pl.pallas_call(
        main_kernel,
        out_shape=[jax.ShapeDtypeStruct(s, f32) for s in out_shapes],
        grid_spec=pltpu.PrefetchScalarGridSpec(
            num_scalar_prefetch=1,
            grid=(CX,),
            in_specs=[plane] * 8
            + [pl.BlockSpec((1, CY, CZ), lambda i, b: (CX - 1, 0, 0))]
            + [whole(s) for s in face_shapes]
            + [
                pl.BlockSpec((1, 16, 128), lambda i, b: (b[0], 0, 0)),
                pl.BlockSpec((1, 16, 128), lambda i, b: (lax.rem(b[0] + 1, 128), 0, 0)),
                whole((32, 128)),
            ],
            out_specs=[plane] * 3 + [whole(s) for s in out_shapes[3:]],
            scratch_shapes=[
                pltpu.VMEM((2048, 128), i32), pltpu.VMEM((32, 128), i32), pltpu.VMEM((16, 128), i32),
                pltpu.VMEM((2, CY, CZ), f32), pltpu.VMEM((4, CX, CZ), f32), pltpu.VMEM((CY, 128), f32),
                plane_scratch, plane_scratch, plane_scratch,
                pltpu.VMEM((128, CY * CZ), f8), pltpu.VMEM((32 * DIGITS, CY * CZ), f8),
                pltpu.VMEM((128, 32 * DIGITS), f32), pltpu.VMEM((256, 4096), f32), pltpu.VMEM((32, 128), f32),
            ],
        ),
        compiler_params=pltpu.CompilerParams(
            dimension_semantics=("arbitrary",), vmem_limit_bytes=58 << 20
        ),
        cost_estimate=pl.CostEstimate(flops=10 ** 9, bytes_accessed=25 << 20, transcendentals=0),
    )(
        block, faces[13], faces[14], conc, adj, solid, load, adj_load, slot, vx,
        *faces[:12], faces[12].reshape(2048, 128), home, home, slot_grain,
    )


def finish_kernel(
    adj1, base, solid, vx, vy, vz, dense, ly, lz, cx, cy, cz,
    out, grad,
    lb, fb, sb, vxb, vyb, vzb, qx, yc, zc,
    xlo, xhi, ylo, yhi, zlo, zhi, d1, r1, r2, s2, r3, s3, r4, lsem, ssem, rsem,
):
    gx, gy, gz = (lax.axis_index(a) for a in ("gx", "gy", "gz"))
    xh, core = gx // 2, lax.rem(gx, 2)
    has = lambda cond: jnp.where(cond, 1.0, 0.0).astype(f32)
    hi_x, hi_y, hi_z = has(gx < 3), has(gy < 7), has(gz < 3)
    keep = pltpu.make_async_copy(dense.at[:, core], d1, lsem.at[0])
    keep.start()
    loads = [
        pltpu.make_async_copy(ref, buf, lsem.at[1 + k])
        for k, (ref, buf) in enumerate(
            ((adj1, lb), (base, fb), (solid, sb), (vx, vxb), (vy, vyb), (vz, vzb))
        )
    ]
    for copy in loads:
        copy.start()
    greet()
    started = []
    send = sender(started, ssem, rsem)
    first = send(dense.at[:, 1 - core], r1, {"gx": gx + 1 - 2 * core})
    faces = [
        send(adj1.at[CX - 1], xlo, {"gx": lax.rem(gx + 1, 4)}),
        send(adj1.at[0], xhi, {"gx": lax.rem(gx + 3, 4)}),
        send(ly.at[1], ylo, {"gy": lax.rem(gy + 1, 8)}),
        send(ly.at[0], yhi, {"gy": lax.rem(gy + 7, 8)}),
        send(lz, zlo, {"gz": lax.rem(gz + 1, 4)}),
        send(lz, zhi, {"gz": lax.rem(gz + 3, 4)}),
    ]
    keep.wait()
    first.wait_recv()

    def add_first(h, carry):
        for x in range(2):
            d1[x, h] = d1[x, h] + r1[x, h]
        return carry

    lax.fori_loop(0, 8, add_first, 0)
    second = [
        send(d1.at[:, lax.rem(gy + o, 8)], r2.at[o - 1], {"gy": lax.rem(gy + o, 8)})
        for o in range(1, 8)
    ]
    for copy in loads:
        copy.wait()
    for copy in faces:
        copy.wait_recv()
    fb[0] = fb[0] + cx[0] * (xlo[...] - lb[0])
    fb[CX - 1] = fb[CX - 1] + cx[1] * (xhi[...] * hi_x) - cx[2] * lb[CX - 1]
    yc[0] = cy[0] * (ylo[...] - ly[0])
    yc[1] = cy[1] * (yhi[...] * hi_y) - cy[2] * ly[1]
    lane1 = lax.broadcasted_iota(i32, (CY, 128), 1)
    own, coef = lz[...], cz[...]
    zc[...] = jnp.where(
        lane1 < 32,
        coef * (pltpu.roll(zlo[...], 96, 1) - own),
        coef * (pltpu.roll(zhi[...], 32, 1) * hi_z) - pltpu.roll(coef, 96, 1) * own,
    )
    qx[...] = jnp.zeros_like(qx)

    def plane(x, carry):
        ri, li, lane = plane_iotas()
        up_y, down_y, up_z, down_z = shifts(ri, li)
        at = pl.ds(x, 1)
        nx = jnp.minimum(x + 1, CX - 1)
        inside = jnp.where(x < CX - 1, 1.0, 0.0).astype(f32)
        l, w = lb[x], weight_of(sb[x])
        a, b = pair(w, weight_of(sb[nx]) * inside, vxb[x])
        d = lb[nx] * inside - l
        lap = fb[x] + b * d - qx[...]
        qx[...] = a * d
        a, b = pair(w, up_y(w), vyb[x])
        d = up_y(l) - l
        lap = lap + b * d - down_y(a * d)
        a, b = pair(w, up_z(w), vzb[x])
        d = up_z(l) - l
        lap = lap + b * d - down_z(a * d)
        cols = zc[...]
        low = pltpu.roll(cols, lax.rem(128 - x, 128), 1)
        high = pltpu.roll(cols, 95 - x, 1)
        lap = lap + jnp.concatenate(
            [jnp.where(lane == 0, low, 0.0), jnp.where(lane == 127, high, 0.0)], axis=1
        )
        fb[x] = lap
        fb[x, 0:1, :] = lap[0:1, :] + yc[0, at, :]
        fb[x, CY - 1:CY, :] = lap[CY - 1:CY, :] + yc[1, at, :]
        return carry

    lax.fori_loop(0, 16, plane, 0)
    store = [pltpu.make_async_copy(fb.at[0:16], out.at[0:16], lsem.at[7])]
    store[0].start()
    for copy in second:
        copy.wait_recv()
    for x in range(2):
        acc = d1[x, gy]
        for o in range(7):
            acc = acc + r2[o, x]
        s2[x] = acc
    third = [
        send(s2.at[:, lax.rem(gz + o, 4)], r3.at[o - 1], {"gz": lax.rem(gz + o, 4)})
        for o in range(1, 4)
    ]
    lax.fori_loop(16, 24, plane, 0)
    for copy in third:
        copy.wait_recv()
    for x in range(2):
        s3[x] = s2[x, gz] + r3[0, x] + r3[1, x] + r3[2, x]
    last = send(s3.at[1 - xh], r4, {"gx": gx + 2 - 4 * xh})
    lax.fori_loop(24, CX, plane, 0)
    store.append(pltpu.make_async_copy(fb.at[16:32], out.at[16:32], lsem.at[8]))
    store[1].start()
    last.wait_recv()
    grad[...] = s3[xh] + r4[...]
    for copy in started:
        copy.wait_send()
    for copy in store:
        copy.wait()


def call_finish(adj1, base, solid, vx, vy, vz, dense, ly, lz, cx, cy, cz):
    vmem = pl.BlockSpec(memory_space=pltpu.VMEM)
    whole = pltpu.VMEM((CX, CY, CZ), f32)
    return pl.pallas_call(
        finish_kernel,
        out_shape=(
            jax.ShapeDtypeStruct((CX, CY, CZ), f32), jax.ShapeDtypeStruct((16, 128), f32)
        ),
        in_specs=[ANY] * 7 + [vmem] * 5,
        out_specs=(ANY, vmem),
        scratch_shapes=[
            whole, whole, pltpu.VMEM((CX, CY, CZ), i32), whole, whole, whole,
            pltpu.VMEM((CY, CZ), f32), pltpu.VMEM((2, CX, CZ), f32), pltpu.VMEM((CY, 128), f32),
            pltpu.VMEM((CY, CZ), f32), pltpu.VMEM((CY, CZ), f32),
            pltpu.VMEM((CX, CZ), f32), pltpu.VMEM((CX, CZ), f32),
            pltpu.VMEM((CY, 128), f32), pltpu.VMEM((CY, 128), f32),
            pltpu.VMEM((2, 8, 4, 16, 128), f32), pltpu.VMEM((2, 8, 4, 16, 128), f32),
            pltpu.VMEM((7, 2, 4, 16, 128), f32), pltpu.VMEM((2, 4, 16, 128), f32),
            pltpu.VMEM((3, 2, 16, 128), f32), pltpu.VMEM((2, 16, 128), f32),
            pltpu.VMEM((16, 128), f32),
            pltpu.SemaphoreType.DMA((9,)), pltpu.SemaphoreType.DMA((18,)),
            pltpu.SemaphoreType.DMA((18,)),
        ],
        compiler_params=pltpu.CompilerParams(
            collective_id=1, has_side_effects=True, vmem_limit_bytes=62 << 20
        ),
    )(adj1, base, solid, vx, vy, vz, dense, ly, lz, cx, cy, cz)


def per_device(
    conc, load, adj_conc, adj_load, vel_x, vel_y, vel_z, solid, voxel_slot, slot_grain, grain_home, rates
):
    block = (lax.axis_index("gx") * 32 + lax.axis_index("gy") * 4 + lax.axis_index("gz")).astype(i32)
    faces = call_faces(conc, adj_conc, vel_x, vel_y, vel_z, solid, rates.reshape(16, 128))
    arrays = (conc, load, adj_conc, adj_load, vel_x, solid, voxel_slot)
    adj1, base, load_start, dense, ly, lz, cx, cy, cz = call_main(
        block.reshape(1), arrays, faces, grain_home.reshape(128, 16, 128), slot_grain.reshape(32, 128)
    )
    start, grad = call_finish(
        adj1, base, solid, vel_x, vel_y, vel_z, dense.reshape(2, 2, 8, 4, 16, 128), ly, lz, cx, cy, cz
    )
    return start, load_start, grad.reshape(2048)


def solution(mesh):
    cells = P("gx", "gy", "gz")
    every = P(("gx", "gy", "gz"))
    return jax.shard_map(
        per_device,
        mesh=mesh,
        in_specs=(cells,) * 9 + (P(("gx", "gy", "gz"), None), P(), every),
        out_specs=(cells, cells, every),
        check_vma=False,
    )
```

time: 138 us -> 119 us (0.86)
  Pallas kernels: 133 us -> 113 us
    pallas_call x1, Pallas kernels: 85.6 us -> 62.5 us  [call_main(): pl.pallas_call(main_kernel, out_shape=[jax.ShapeDtypeStruct(s, f32) for s...]
    pallas_call x1, Pallas kernels: 26.4 us -> 28.5 us  [call_faces(): pl.pallas_call(gather_faces, out_shape=outs, in_specs=[ANY] * 7, out_spec...]
    pallas_call x1, Pallas kernels: 20.7 us -> 22.3 us  [call_finish(): pl.pallas_call(finish_kernel, out_shape=(jax.ShapeDtypeStruct((CX, CY, CZ...]
where the time goes in v3:
time: 119 us; the launch traced here: 118 us
  Pallas kernels  113 us (95%)
  local copies, waits for them, and re-layouts  3.74 us (3%)
    pallas_call x1, Pallas kernels, call_main(): pl.pallas_call(main_kernel, out_shape=[jax.ShapeDtypeStruct(s, f32) for s...  62.5 us
    pallas_call x1, Pallas kernels, call_faces(): pl.pallas_call(gather_faces, out_shape=outs, in_specs=[ANY] * 7, out_spec...  28.5 us
    pallas_call x1, Pallas kernels, call_finish(): pl.pallas_call(finish_kernel, out_shape=(jax.ShapeDtypeStruct((CX, CY, CZ...  22.3 us
    unnamed x4, local copies, waits for them, and re-layouts  3.74 us

profile of v3, /device:TPU:1, one launch (start us, length us, event | category | flops | bytes accessed | tf_op | source)
XLA Modules:
  0.0 117.7 jit_solution(11791805804835620340)
XLA Ops:
  0.6 28.5 %shard_map.139 = (f32[3,64,256]{2,1,0:T(8,128)}, s32[64,256]{1,0:T(8,128)}, f32[2,64,256]{2,1,0:T(8,128)}, s32[64,256]{1,0:T(8,128)}, f32[4,32,256]{2,1,0:T(8,12...) custom-call(f32[32,64,256]{2,1,0:T(8,128)} %conc_ref.1, ...), custom_call_target="tpu_custom_call" | custom-call | tf_op jit(solution)/shard_map/pallas_call | solution.py:215
  29.2 62.5 %shard_map.140 = (f32[32,64,256]{2,1,0:T(8,128)}, f32[32,64,256]{2,1,0:T(8,128)}, f32[32,64,256]{2,1,0:T(8,128)}, f32[2048,128]{1,0:T(8,128)}, f32[2,32,256]{2,1...) custom-call(s32[1]{0:T(128)} %bitcast.block_ref, ...), custom_call_target="tpu_custom_call" | custom-call | flops 1000000000 | bytes 26214400 | tf_op jit(solution)/shard_map/pallas_call | solution.py:527
  91.7 22.3 %shard_map.141 = (f32[32,64,256]{2,1,0:T(8,128)}, f32[16,128]{1,0:T(8,128)}) custom-call(f32[32,64,256]{2,1,0:T(8,128)} %get-tuple-element.44.adj1, f32[32,64,256]{2,1,0:T(8,128)} %get-tuple-element.45.base, s32[32,64,256]{2,1,0:T(8,128)} %solid.3, f32[32,64,256]{2,1,0:T(8,128)} %vx.3, f32[32,64,256]{2,1,0:T(8,128)} %vy.3, f32[32,64,256]{2,1,0:T(8,128)} %vz.3, ...), custom_call_target="tpu_custom_call" | custom-call | tf_op jit(solution)/shard_map/pallas_call | solution.py:684
  114.0 0.0 copy-start
  114.0 3.1 %copy.17 = f32[32,64,256]{2,1,0:T(8,128)} copy(f32[32,64,256]{2,1,0:T(8,128)} %get-tuple-element.58) | data formatting | bytes 4194304
  117.1 0.0 copy-done
  117.1 0.6 copy.18
Async XLA Ops:
  114.0 3.1 %copy-start = (f32[16,128]{1,0:T(8,128)S(1)}, f32[16,128]{1,0:T(8,128)}, u32[]{:S(2)}) copy-start(f32[16,128]{1,0:T(8,128)} %get-tuple-element.54) | copy-start | bytes 24580

commit v4 on v3

--- a/solution.py
+++ b/solution.py
@@ -10,6 +10,7 @@
 f32, bf16, i32, f8 = jnp.float32, jnp.bfloat16, jnp.int32, jnp.float8_e4m3fn
 DIGITS = 3
 CHUNKS = 4
+PLANES = 2
 MESH = pl.DeviceIdType.MESH
 ANY = pl.BlockSpec(memory_space=pl.ANY)
 dispersion = 0.06
@@ -55,17 +56,23 @@
 
 
 def sender(started, ssem, rsem):
-    def send(src, dst, where):
-        k = len(started)
+    def send(src, dst, where, slot=None):
+        k = len(started) if slot is None else slot
         copy = pltpu.make_async_remote_copy(
             src_ref=src, dst_ref=dst, send_sem=ssem.at[k], recv_sem=rsem.at[k],
             device_id=where, device_id_type=MESH,
         )
-        copy.start()
-        started.append(copy)
+        if slot is None:
+            copy.start()
+            started.append(copy)
         return copy
 
     return send
+
+
+def each(copies, what):
+    for copy in copies:
+        getattr(copy, what)()
 
 
 def gather_faces(
@@ -152,24 +159,41 @@
 
     mine.wait()
     first.wait_recv()
-    second = [
-        send(rall.at[:, core, gy, gz], rall.at[:, core, gy, gz], {"gz": lax.rem(gz + o, 4)})
-        for o in range(1, 4)
-    ]
+    one, row_y, row_z = rall.at[:, core, gy, gz], rall.at[:, core, gy], rall.at[:, core, :, gz]
+    to_z = [{"gz": lax.rem(gz + o, 4)} for o in range(1, 4)]
+    to_y = [{"gy": lax.rem(gy + o, 8)} for o in range(1, 8)]
+    second = (
+        [send(one, one, where, 13 + n) for n, where in enumerate(to_z)],
+        [send(one, one, where, 16 + n) for n, where in enumerate(to_y)],
+    )
+    third = (
+        [send(row_y, row_y, where, 23 + n) for n, where in enumerate(to_y)],
+        [send(row_z, row_z, where, 30 + n) for n, where in enumerate(to_z)],
+    )
+    for way in range(2):
+        @pl.when(core == way)
+        def _():
+            each(second[way], "start")
+
     arrived(0)
     arrived(1)
     lax.fori_loop(0, 5, plane, 0)
-    for copy in second:
-        copy.wait_recv()
-    third = [
-        send(rall.at[:, core, gy], rall.at[:, core, gy], {"gy": lax.rem(gy + o, 8)})
-        for o in range(1, 8)
-    ]
+    for way in range(2):
+        @pl.when(core == way)
+        def _():
+            each(second[way], "wait_recv")
+            each(third[way], "start")
+
     arrived(2)
     arrived(3)
     lax.fori_loop(5, 24, plane, 0)
-    for copy in third:
-        copy.wait_recv()
+    for way in range(2):
+        @pl.when(core == way)
+        def _():
+            each(third[way], "wait_recv")
+            each(second[way], "wait_send")
+            each(third[way], "wait_send")
+
     last = send(rall.at[:, core], rall.at[:, core], {"gx": gx + 1 - 2 * core})
     outs = [
         pltpu.make_async_copy(s1.at[0:24], s1_out.at[0:24], osem.at[1]),
@@ -222,8 +246,8 @@
             pltpu.VMEM((CY, CZ), f32), pltpu.VMEM((CY, CZ), f32),
             pltpu.VMEM((4, CX, CZ), f32), pltpu.VMEM((3, CX, CZ), f32),
             pltpu.VMEM((CY, 128), f32), pltpu.VMEM((CY, 128), f32),
-            pltpu.SemaphoreType.DMA((24,)), pltpu.SemaphoreType.DMA((23,)),
-            pltpu.SemaphoreType.DMA((9,)), pltpu.SemaphoreType.DMA((23,)),
+            pltpu.SemaphoreType.DMA((24,)), pltpu.SemaphoreType.DMA((33,)),
+            pltpu.SemaphoreType.DMA((9,)), pltpu.SemaphoreType.DMA((33,)),
         ],
         compiler_params=pltpu.CompilerParams(
             collective_id=0, has_side_effects=True, vmem_limit_bytes=62 << 20
@@ -243,17 +267,20 @@
     packed, places_ref, table, xc, yc, zc,
     hi_f, lo_f, term_f, hot_lo, hot_hi, total, got_ref, look_ref,
 ):
-    i = pl.program_id(0)
+    step = pl.program_id(0)
     gx, gy, gz = (lax.axis_index(a) for a in ("gx", "gy", "gz"))
     has = lambda cond: jnp.where(cond, 1.0, 0.0).astype(f32)
     lo_x, hi_x = has(gx > 0), has(gx < 3)
     lo_y, hi_y = has(gy > 0), has(gy < 7)
     lo_z, hi_z = has(gz > 0), has(gz < 3)
     lane1 = lax.broadcasted_iota(i32, (CY, 128), 1)
-    @pl.when(i == 0)
+    @pl.when(step == 0)
     def _():
         total[...] = jnp.zeros_like(total)
         hot_lo[...] = jnp.zeros_like(hot_lo)
+        term_f[...] = jnp.zeros_like(term_f)
+        hi_f[...] = jnp.zeros_like(hi_f)
+        lo_f[...] = jnp.zeros_like(lo_f)
         hot_hi[...] = jnp.zeros_like(hot_hi)
         def pack(r, carry):
             at = pl.ds(pl.multiple_of(r * 128, 128), 128)
@@ -313,6 +340,8 @@
         a, b = pair(weight_of(xlo_s[...]) * lo_x, weight_of(solid_ref[0]), xlo[2] * lo_x)
         xc[0] = b * (xlo[0] * lo_x) - a * conc_ref[0]
         xc[1] = a * (xlo[1] * lo_x - adj_ref[0])
+        xc[2] = xc[0]
+        xc[3] = xc[1]
         cx_ref[0] = a
         a, b = pair(ylo[3] * lo_y, yown[2], ylo[2] * lo_y)
         yc[0] = b * (ylo[0] * lo_y) - a * yown[0]
@@ -346,51 +375,46 @@
         cz_ref[...] = lay([coef, b, k, jnp.zeros_like(k)])
         lz_ref[...] = jnp.zeros_like(lz_ref)
 
-    @pl.when(i == CX - 1)
+    @pl.when(step == CX // PLANES - 1)
     def _():
-        k = (dispersion * weight_of(solid_ref[0])) * (weight_of(xhi_s[...]) * hi_x)
+        k = (dispersion * weight_of(solid_ref[PLANES - 1])) * (weight_of(xhi_s[...]) * hi_x)
         v = vend_ref[0]
         a, b = k - jnp.minimum(v, 0.0), k + jnp.maximum(v, 0.0)
-        xc[0] = a * (xhi[0] * hi_x) - k * conc_ref[0]
-        xc[1] = b * (xhi[1] * hi_x) - k * adj_ref[0]
+        xc[2] = a * (xhi[0] * hi_x) - k * conc_ref[PLANES - 1]
+        xc[3] = b * (xhi[1] * hi_x) - k * adj_ref[PLANES - 1]
         cx_ref[1] = b
         cx_ref[2] = k
 
-    def products():
-        acc = None
-        for chunk in range(CHUNKS):
-            span = slice(chunk * (CY * CZ // CHUNKS), (chunk + 1) * (CY * CZ // CHUNKS))
-            got = lax.dot_general(
-                hot_lo[:, span], hot_hi[:, span], (((1,), (1,)), ((), ())), preferred_element_type=f32
-            )
-            acc = got if acc is None else acc + got
-        return acc
-
-    total[...] = total[...] + products()
-    at = pl.ds(i, 1)
-    end = i == CX - 1
-    ri = lax.broadcasted_iota(i32, (8, CZ), 0)
-    edge = jnp.where((i == 0) | end, 1.0, 0.0).astype(f32)
-
-    def with_faces(v, n):
-        v = v + edge * xc[n]
-        low = roll_tile(zc[...], lax.rem(256 - i - 32 * n, 128))
-        high = roll_tile(zc[...], lax.rem(319 - i - 32 * n, 128))
-        v = v + jnp.concatenate(
-            [jnp.where(lane1 == 0, low, 0.0), jnp.where(lane1 == 127, high, 0.0)], axis=1
+    ids = lax.broadcasted_iota(i32, (128, CZ), 0).astype(f32).astype(bf16)
+    zero, one = jnp.zeros((32, CZ), bf16), jnp.ones((32, CZ), bf16)
+    rows_of = CY // CHUNKS
+    width = rows_of * CZ
+
+    def product(g):
+        span = slice(g * width, (g + 1) * width)
+        return lax.dot_general(
+            hot_lo[:, span], hot_hi[:, span], (((1,), (1,)), ((), ())), preferred_element_type=f32
         )
-        first = v[0:8, :] + jnp.where(ri == 0, yc[n, at, :], 0.0)
-        final = v[CY - 8:CY, :] + jnp.where(ri == 7, yc[2 + n, at, :], 0.0)
-        return jnp.concatenate([first, v[8:CY - 8, :], final], axis=0)
-
-    c, l = conc_ref[0], adj_ref[0]
-    sol = solid_ref[0].astype(f32)
-
-    lookups = []
-    for g in range(CY // 8):
+
+    def make_hot(g):
+        def row(plane):
+            half = jnp.broadcast_to(plane, (16, CZ)).astype(bf16)
+            return jnp.concatenate([half, half], axis=0)
+
+        for y in range(g * rows_of, (g + 1) * rows_of):
+            span = slice(y * CZ, y * CZ + CZ)
+            mask = ids[0:32] == row(hi_f[y:y + 1, :])
+            for k in range(DIGITS):
+                hot_hi[32 * k:32 * k + 32, span] = jnp.where(mask, row(term_f[k, y:y + 1, :]), zero).astype(f8)
+            low = row(lo_f[y:y + 1, :])
+            for j in range(4):
+                at_j = slice(32 * j, 32 * j + 32)
+                hot_lo[at_j, span] = jnp.where(ids[at_j] == low, one, zero).astype(f8)
+
+    def rate_of(p, g):
         halves = []
         for h in range(2):
-            s = slot_ref[0, 8 * g:8 * g + 8, 128 * h:128 * h + 128]
+            s = slot_ref[p, 8 * g:8 * g + 8, 128 * h:128 * h + 128]
             lo, hi = s & 127, s >> 7
             level = [
                 jnp.take_along_axis(jnp.broadcast_to(table[r:r + 1, :], (8, 128)), lo, axis=1)
@@ -401,61 +425,88 @@
                 level = [
                     jnp.where(mask, level[2 * j + 1], level[2 * j]) for j in range(len(level) // 2)
                 ]
-            p = level[0]
-            value = jnp.where((hi & 16) != 0, lax.shift_right_logical(p, 16), p & 65535)
+            both = level[0]
+            value = jnp.where((hi & 16) != 0, lax.shift_right_logical(both, 16), both & 65535)
             halves.append(value.astype(f32) * rate_step)
-        lookups.append(jnp.concatenate(halves, axis=1))
-    kv = sol * jnp.concatenate(lookups, axis=0)
-
-    def inverse(v):
-        r = pl.reciprocal(v, approx=True)
-        return r * (2.0 - v * r)
-
-    m = adjload_ref[0]
-    u0 = inverse(1.0 + c)
-    e0 = c * u0 - load_ref[0]
-    r = kv * e0
-    conc1 = with_faces(s1_ref[0], 0) - r
-    load1 = load_ref[0] + r
-    d1 = m - l
-    u1 = inverse(1.0 + conc1)
-    kd = kv * d1
-    adj1 = with_faces(s2_ref[0], 1) + kd * (u1 * u1)
-    m1 = m - kd
-    d0 = m1 - adj1
-    kd = kv * d0
-    mstart_ref[0] = m1 - kd
-    term_f[...] = sol * ((conc1 * u1 - load1) * d1 + e0 * d0)
-    base_ref[0] = adj1 + kd * (u0 * u0)
-    adj1_ref[0] = adj1
-    ly_ref[0, at, :] = adj1[0:1, :]
-    ly_ref[1, at, :] = adj1[CY - 1:CY, :]
-    packed_l = jnp.where(lane1 == i, adj1[:, 0:1], lz_ref[...])
-    lz_ref[...] = jnp.where(lane1 == i + 32, adj1[:, CZ - 1:CZ], packed_l)
-
-    slots = slot_ref[0]
-    hi_f[...] = (slots >> 7).astype(f32)
-    lo_f[...] = (slots & 127).astype(f32)
-    ids = lax.broadcasted_iota(i32, (128, CZ), 0).astype(f32).astype(bf16)
-    zero, one = jnp.zeros((32, CZ), bf16), jnp.ones((32, CZ), bf16)
-    row = lambda ref, y: jnp.broadcast_to(ref[y:y + 1, :], (32, CZ))
-    for y in range(CY):
-        span = slice(y * CZ, y * CZ + CZ)
-        rest = row(term_f, y)
-        mask = ids[0:32] == row(hi_f, y).astype(bf16)
+        return jnp.concatenate(halves, axis=1)
+
+    def one_plane(p):
+        i = step * PLANES + p
+        acc = total[...]
+        lookups = []
+        per = CY // 8 // CHUNKS
+        for g in range(CHUNKS):
+            acc = acc + product(g)
+            for n in range(per):
+                lookups.append(rate_of(p, g * per + n))
+            make_hot(g)
+        total[...] = acc
+        at = pl.ds(i, 1)
+        end = i == CX - 1
+        ri = lax.broadcasted_iota(i32, (8, CZ), 0)
+        edge = jnp.where((i == 0) | end, 1.0, 0.0).astype(f32)
+        edge_at = 0 if p == 0 else 2
+
+        def with_faces(v, n):
+            v = v + edge * xc[edge_at + n]
+            low = roll_tile(zc[...], lax.rem(256 - i - 32 * n, 128))
+            high = roll_tile(zc[...], lax.rem(319 - i - 32 * n, 128))
+            v = v + jnp.concatenate(
+                [jnp.where(lane1 == 0, low, 0.0), jnp.where(lane1 == 127, high, 0.0)], axis=1
+            )
+            first = v[0:8, :] + jnp.where(ri == 0, yc[n, at, :], 0.0)
+            final = v[CY - 8:CY, :] + jnp.where(ri == 7, yc[2 + n, at, :], 0.0)
+            return jnp.concatenate([first, v[8:CY - 8, :], final], axis=0)
+
+        c, l = conc_ref[p], adj_ref[p]
+        sol = solid_ref[p].astype(f32)
+
+        kv = sol * jnp.concatenate(lookups, axis=0)
+
+        def inverse(v):
+            r = pl.reciprocal(v, approx=True)
+            return r * (2.0 - v * r)
+
+        m = adjload_ref[p]
+        u0 = inverse(1.0 + c)
+        e0 = c * u0 - load_ref[p]
+        r = kv * e0
+        conc1 = with_faces(s1_ref[p], 0) - r
+        load1 = load_ref[p] + r
+        d1 = m - l
+        u1 = inverse(1.0 + conc1)
+        kd = kv * d1
+        adj1 = with_faces(s2_ref[p], 1) + kd * (u1 * u1)
+        m1 = m - kd
+        d0 = m1 - adj1
+        kd = kv * d0
+        mstart_ref[p] = m1 - kd
+        rest = sol * ((conc1 * u1 - load1) * d1 + e0 * d0)
         for k in range(DIGITS):
             digit = rest.astype(f8).astype(f32)
-            hot_hi[32 * k:32 * k + 32, span] = jnp.where(mask, digit.astype(bf16), zero).astype(f8)
-            if k < DIGITS - 1:
-                rest = (rest - digit) * 16.0
-        low = row(lo_f, y).astype(bf16)
-        for j in range(4):
-            at_j = slice(32 * j, 32 * j + 32)
-            hot_lo[at_j, span] = jnp.where(ids[at_j] == low, one, zero).astype(f8)
-
-    @pl.when(end)
+            term_f[k] = digit
+            rest = (rest - digit) * 16.0
+        base_ref[p] = adj1 + kd * (u0 * u0)
+        adj1_ref[p] = adj1
+        ly_ref[0, at, :] = adj1[0:1, :]
+        ly_ref[1, at, :] = adj1[CY - 1:CY, :]
+        packed_l = jnp.where(lane1 == i, adj1[:, 0:1], lz_ref[...])
+        lz_ref[...] = jnp.where(lane1 == i + 32, adj1[:, CZ - 1:CZ], packed_l)
+
+        slots = slot_ref[p]
+        hi_f[...] = (slots >> 7).astype(f32)
+        lo_f[...] = (slots & 127).astype(f32)
+
+    for p in range(PLANES):
+        one_plane(p)
+
+    @pl.when(step == CX // PLANES - 1)
     def _():
-        total[...] = total[...] + products()
+        for g in range(CHUNKS):
+            total[...] = total[...] + product(g)
+            make_hot(g)
+        for g in range(CHUNKS):
+            total[...] = total[...] + product(g)
         by_lane = total[...].T
         sums = by_lane[32 * DIGITS - 32:32 * DIGITS]
         for k in range(DIGITS - 2, -1, -1):
@@ -509,7 +560,7 @@
 
 def call_main(block, arrays, faces, home, slot_grain):
     conc, load, adj, adj_load, vx, solid, slot = arrays
-    plane = pl.BlockSpec((1, CY, CZ), lambda i, b: (i, 0, 0))
+    plane = pl.BlockSpec((PLANES, CY, CZ), lambda i, b: (i, 0, 0))
 
     def whole(shape):
         return pl.BlockSpec(shape, lambda i, b: (0,) * len(shape))
@@ -529,7 +580,7 @@
         out_shape=[jax.ShapeDtypeStruct(s, f32) for s in out_shapes],
         grid_spec=pltpu.PrefetchScalarGridSpec(
             num_scalar_prefetch=1,
-            grid=(CX,),
+            grid=(CX // PLANES,),
             in_specs=[plane] * 8
             + [pl.BlockSpec((1, CY, CZ), lambda i, b: (CX - 1, 0, 0))]
             + [whole(s) for s in face_shapes]
@@ -541,8 +592,8 @@
             out_specs=[plane] * 3 + [whole(s) for s in out_shapes[3:]],
             scratch_shapes=[
                 pltpu.VMEM((2048, 128), i32), pltpu.VMEM((32, 128), i32), pltpu.VMEM((16, 128), i32),
-                pltpu.VMEM((2, CY, CZ), f32), pltpu.VMEM((4, CX, CZ), f32), pltpu.VMEM((CY, 128), f32),
-                plane_scratch, plane_scratch, plane_scratch,
+                pltpu.VMEM((4, CY, CZ), f32), pltpu.VMEM((4, CX, CZ), f32), pltpu.VMEM((CY, 128), f32),
+                plane_scratch, plane_scratch, pltpu.VMEM((DIGITS, CY, CZ), f32),
                 pltpu.VMEM((128, CY * CZ), f8), pltpu.VMEM((32 * DIGITS, CY * CZ), f8),
                 pltpu.VMEM((128, 32 * DIGITS), f32), pltpu.VMEM((256, 4096), f32), pltpu.VMEM((32, 128), f32),
             ],
@@ -561,7 +612,8 @@
     adj1, base, solid, vx, vy, vz, dense, ly, lz, cx, cy, cz,
     out, grad,
     lb, fb, sb, vxb, vyb, vzb, qx, yc, zc,
-    xlo, xhi, ylo, yhi, zlo, zhi, d1, r1, r2, s2, r3, s3, r4, lsem, ssem, rsem,
+    xlo, xhi, ylo, yhi, zlo, zhi, d1, r1, r2y, r2z, s2y, s2z, r3z, r3y, s3, r4,
+    lsem, ssem, rsem,
 ):
     gx, gy, gz = (lax.axis_index(a) for a in ("gx", "gy", "gz"))
     xh, core = gx // 2, lax.rem(gx, 2)
@@ -598,10 +650,21 @@
         return carry
 
     lax.fori_loop(0, 8, add_first, 0)
-    second = [
-        send(d1.at[:, lax.rem(gy + o, 8)], r2.at[o - 1], {"gy": lax.rem(gy + o, 8)})
-        for o in range(1, 8)
-    ]
+    ys = [lax.rem(gy + o, 8) for o in range(1, 8)]
+    zs = [lax.rem(gz + o, 4) for o in range(1, 4)]
+    second = (
+        [send(d1.at[:, y], r2y.at[n], {"gy": y}, 8 + n) for n, y in enumerate(ys)],
+        [send(d1.at[:, :, z], r2z.at[n], {"gz": z}, 15 + n) for n, z in enumerate(zs)],
+    )
+    third = (
+        [send(s2y.at[:, z], r3z.at[n], {"gz": z}, 18 + n) for n, z in enumerate(zs)],
+        [send(s2z.at[:, y], r3y.at[n], {"gy": y}, 21 + n) for n, y in enumerate(ys)],
+    )
+    for way in range(2):
+        @pl.when(core == way)
+        def _():
+            each(second[way], "start")
+
     for copy in loads:
         copy.wait()
     for copy in faces:
@@ -650,22 +713,53 @@
     lax.fori_loop(0, 16, plane, 0)
     store = [pltpu.make_async_copy(fb.at[0:16], out.at[0:16], lsem.at[7])]
     store[0].start()
-    for copy in second:
-        copy.wait_recv()
-    for x in range(2):
-        acc = d1[x, gy]
-        for o in range(7):
-            acc = acc + r2[o, x]
-        s2[x] = acc
-    third = [
-        send(s2.at[:, lax.rem(gz + o, 4)], r3.at[o - 1], {"gz": lax.rem(gz + o, 4)})
-        for o in range(1, 4)
-    ]
+    for way in range(2):
+        @pl.when(core == way)
+        def _():
+            each(second[way], "wait_recv")
+
+    @pl.when(core == 0)
+    def _():
+        for x in range(2):
+            acc = d1[x, gy]
+            for o in range(7):
+                acc = acc + r2y[o, x]
+            s2y[x] = acc
+        each(third[0], "start")
+
+    @pl.when(core == 1)
+    def _():
+        for x in range(2):
+            for h in range(8):
+                acc = d1[x, h, gz]
+                for o in range(3):
+                    acc = acc + r2z[o, x, h]
+                s2z[x, h] = acc
+        each(third[1], "start")
+
     lax.fori_loop(16, 24, plane, 0)
-    for copy in third:
-        copy.wait_recv()
-    for x in range(2):
-        s3[x] = s2[x, gz] + r3[0, x] + r3[1, x] + r3[2, x]
+    @pl.when(core == 0)
+    def _():
+        each(third[0], "wait_recv")
+        for x in range(2):
+            acc = s2y[x, gz]
+            for o in range(3):
+                acc = acc + r3z[o, x]
+            s3[x] = acc
+        each(second[0], "wait_send")
+        each(third[0], "wait_send")
+
+    @pl.when(core == 1)
+    def _():
+        each(third[1], "wait_recv")
+        for x in range(2):
+            acc = s2z[x, gy]
+            for o in range(7):
+                acc = acc + r3y[o, x]
+            s3[x] = acc
+        each(second[1], "wait_send")
+        each(third[1], "wait_send")
+
     last = send(s3.at[1 - xh], r4, {"gx": gx + 2 - 4 * xh})
     lax.fori_loop(24, CX, plane, 0)
     store.append(pltpu.make_async_copy(fb.at[16:32], out.at[16:32], lsem.at[8]))
@@ -695,11 +789,12 @@
             pltpu.VMEM((CX, CZ), f32), pltpu.VMEM((CX, CZ), f32),
             pltpu.VMEM((CY, 128), f32), pltpu.VMEM((CY, 128), f32),
             pltpu.VMEM((2, 8, 4, 16, 128), f32), pltpu.VMEM((2, 8, 4, 16, 128), f32),
-            pltpu.VMEM((7, 2, 4, 16, 128), f32), pltpu.VMEM((2, 4, 16, 128), f32),
-            pltpu.VMEM((3, 2, 16, 128), f32), pltpu.VMEM((2, 16, 128), f32),
-            pltpu.VMEM((16, 128), f32),
-            pltpu.SemaphoreType.DMA((9,)), pltpu.SemaphoreType.DMA((18,)),
-            pltpu.SemaphoreType.DMA((18,)),
+            pltpu.VMEM((7, 2, 4, 16, 128), f32), pltpu.VMEM((3, 2, 8, 16, 128), f32),
+            pltpu.VMEM((2, 4, 16, 128), f32), pltpu.VMEM((2, 8, 16, 128), f32),
+            pltpu.VMEM((3, 2, 16, 128), f32), pltpu.VMEM((7, 2, 16, 128), f32),
+            pltpu.VMEM((2, 16, 128), f32), pltpu.VMEM((16, 128), f32),
+            pltpu.SemaphoreType.DMA((9,)), pltpu.SemaphoreType.DMA((28,)),
+            pltpu.SemaphoreType.DMA((28,)),
         ],
         compiler_params=pltpu.CompilerParams(
             collective_id=1, has_side_effects=True, vmem_limit_bytes=62 << 20

time: 119 us -> 106 us (0.89)
  Pallas kernels: 113 us -> 102 us
    pallas_call x1, Pallas kernels: 62.5 us -> 51 us  [call_main(): pl.pallas_call(main_kernel, out_shape=[jax.ShapeDtypeStruct(s, f32) for s...]
    pallas_call x1, Pallas kernels: 22.3 us -> 20.9 us  [call_finish(): pl.pallas_call(finish_kernel, out_shape=(jax.ShapeDtypeStruct((CX, CY, CZ...]
where the time goes in v4:
time: 106 us
  Pallas kernels  102 us (96%)
  local copies, waits for them, and re-layouts  3.74 us (4%)
    pallas_call x1, Pallas kernels, call_main(): pl.pallas_call(main_kernel, out_shape=[jax.ShapeDtypeStruct(s, f32) for s...  51 us
    pallas_call x1, Pallas kernels, call_faces(): pl.pallas_call(gather_faces, out_shape=outs, in_specs=[ANY] * 7, out_spec...  29.5 us
    pallas_call x1, Pallas kernels, call_finish(): pl.pallas_call(finish_kernel, out_shape=(jax.ShapeDtypeStruct((CX, CY, CZ...  20.9 us
    unnamed x4, local copies, waits for them, and re-layouts  3.74 us

profile of v4, /device:TPU:1, one launch (start us, length us, event | category | flops | bytes accessed | tf_op | source)
XLA Modules:
  0.0 105.9 jit_solution(11287435656128955677)
XLA Ops:
  0.6 29.5 %shard_map.139 = (f32[3,64,256]{2,1,0:T(8,128)}, s32[64,256]{1,0:T(8,128)}, f32[2,64,256]{2,1,0:T(8,128)}, s32[64,256]{1,0:T(8,128)}, f32[4,32,256]{2,1,0:T(8,12...) custom-call(f32[32,64,256]{2,1,0:T(8,128)} %conc_ref.1, ...), custom_call_target="tpu_custom_call" | custom-call | tf_op jit(solution)/shard_map/pallas_call | solution.py:239
  30.2 51.0 %shard_map.140 = (f32[32,64,256]{2,1,0:T(8,128)}, f32[32,64,256]{2,1,0:T(8,128)}, f32[32,64,256]{2,1,0:T(8,128)}, f32[2048,128]{1,0:T(8,128)}, f32[2,32,256]{2,1...) custom-call(s32[1]{0:T(128)} %bitcast.block_ref, ...), custom_call_target="tpu_custom_call" | custom-call | flops 1000000000 | bytes 26214400 | tf_op jit(solution)/shard_map/pallas_call | solution.py:578
  81.2 20.9 %shard_map.141 = (f32[32,64,256]{2,1,0:T(8,128)}, f32[16,128]{1,0:T(8,128)}) custom-call(f32[32,64,256]{2,1,0:T(8,128)} %get-tuple-element.44.adj1, f32[32,64,256]{2,1,0:T(8,128)} %get-tuple-element.45.base, s32[32,64,256]{2,1,0:T(8,128)} %solid.3, f32[32,64,256]{2,1,0:T(8,128)} %vx.3, f32[32,64,256]{2,1,0:T(8,128)} %vy.3, f32[32,64,256]{2,1,0:T(8,128)} %vz.3, ...), custom_call_target="tpu_custom_call" | custom-call | tf_op jit(solution)/shard_map/pallas_call | solution.py:778
  102.2 0.0 copy-start
  102.2 3.1 %copy.17 = f32[32,64,256]{2,1,0:T(8,128)} copy(f32[32,64,256]{2,1,0:T(8,128)} %get-tuple-element.58) | data formatting | bytes 4194304
  105.3 0.0 copy-done
  105.3 0.6 copy.18
Async XLA Ops:
  102.2 3.1 %copy-start = (f32[16,128]{1,0:T(8,128)S(1)}, f32[16,128]{1,0:T(8,128)}, u32[]{:S(2)}) copy-start(f32[16,128]{1,0:T(8,128)} %get-tuple-element.54) | copy-start | bytes 24580

commit v5 on v4

--- a/solution.py
+++ b/solution.py
@@ -26,7 +26,16 @@
             pl.semaphore_signal(
                 barrier, inc=1, device_id={axis: lax.rem(me + o, count)}, device_id_type=MESH
             )
-    pl.semaphore_wait(barrier, 13)
+    gx = lax.axis_index("gx")
+    across = gx + 2 - 4 * (gx // 2)
+    for axis, count in (("gy", 8), ("gz", 4)):
+        me = lax.axis_index(axis)
+        for o in range(1, count):
+            pl.semaphore_signal(
+                barrier, inc=1, device_id={"gx": across, axis: lax.rem(me + o, count)},
+                device_id_type=MESH,
+            )
+    pl.semaphore_wait(barrier, 23)
 
 
 def weight_of(s):
@@ -99,7 +108,28 @@
 
     started = []
     send = sender(started, ssem, rsem)
-    first = send(rates, rall.at[xh, core, gy, gz], {"gx": gx + 2 - 4 * xh})
+    one, row_y, row_z = rall.at[xh, core, gy, gz], rall.at[:, core, gy], rall.at[:, core, :, gz]
+    near = [(dx, o) for dx in range(2) for o in range(8) if dx + o > 0]
+    side = lambda dx: gx + dx * (2 - 4 * xh)
+    second = (
+        [
+            send(rates, one, {"gx": side(dx), "gz": lax.rem(gz + o, 4)}, 12 + n)
+            for n, (dx, o) in enumerate([p for p in near if p[1] < 4])
+        ],
+        [
+            send(rates, one, {"gx": side(dx), "gy": lax.rem(gy + o, 8)}, 19 + n)
+            for n, (dx, o) in enumerate(near)
+        ],
+    )
+    third = (
+        [send(row_y, row_y, {"gy": lax.rem(gy + o, 8)}, 33 + o) for o in range(1, 8)],
+        [send(row_z, row_z, {"gz": lax.rem(gz + o, 4)}, 40 + o) for o in range(1, 4)],
+    )
+    for way in range(2):
+        @pl.when(core == way)
+        def _():
+            each(second[way], "start")
+
     right, left = {"gx": lax.rem(gx + 1, 4)}, {"gx": lax.rem(gx + 3, 4)}
     faces = []
     for k, ref in enumerate((conc, adj, vx)):
@@ -158,23 +188,6 @@
             copy.wait()
 
     mine.wait()
-    first.wait_recv()
-    one, row_y, row_z = rall.at[:, core, gy, gz], rall.at[:, core, gy], rall.at[:, core, :, gz]
-    to_z = [{"gz": lax.rem(gz + o, 4)} for o in range(1, 4)]
-    to_y = [{"gy": lax.rem(gy + o, 8)} for o in range(1, 8)]
-    second = (
-        [send(one, one, where, 13 + n) for n, where in enumerate(to_z)],
-        [send(one, one, where, 16 + n) for n, where in enumerate(to_y)],
-    )
-    third = (
-        [send(row_y, row_y, where, 23 + n) for n, where in enumerate(to_y)],
-        [send(row_z, row_z, where, 30 + n) for n, where in enumerate(to_z)],
-    )
-    for way in range(2):
-        @pl.when(core == way)
-        def _():
-            each(second[way], "start")
-
     arrived(0)
     arrived(1)
     lax.fori_loop(0, 5, plane, 0)
@@ -246,8 +259,8 @@
             pltpu.VMEM((CY, CZ), f32), pltpu.VMEM((CY, CZ), f32),
             pltpu.VMEM((4, CX, CZ), f32), pltpu.VMEM((3, CX, CZ), f32),
             pltpu.VMEM((CY, 128), f32), pltpu.VMEM((CY, 128), f32),
-            pltpu.SemaphoreType.DMA((24,)), pltpu.SemaphoreType.DMA((33,)),
-            pltpu.SemaphoreType.DMA((9,)), pltpu.SemaphoreType.DMA((33,)),
+            pltpu.SemaphoreType.DMA((24,)), pltpu.SemaphoreType.DMA((44,)),
+            pltpu.SemaphoreType.DMA((9,)), pltpu.SemaphoreType.DMA((44,)),
         ],
         compiler_params=pltpu.CompilerParams(
             collective_id=0, has_side_effects=True, vmem_limit_bytes=62 << 20
@@ -612,7 +625,7 @@
     adj1, base, solid, vx, vy, vz, dense, ly, lz, cx, cy, cz,
     out, grad,
     lb, fb, sb, vxb, vyb, vzb, qx, yc, zc,
-    xlo, xhi, ylo, yhi, zlo, zhi, d1, r1, r2y, r2z, s2y, s2z, r3z, r3y, s3, r4,
+    xlo, xhi, ylo, yhi, zlo, zhi, d1, r1, r2y, r2z, s2y, s2z, r3z, r3y,
     lsem, ssem, rsem,
 ):
     gx, gy, gz = (lax.axis_index(a) for a in ("gx", "gy", "gz"))
@@ -650,15 +663,24 @@
         return carry
 
     lax.fori_loop(0, 8, add_first, 0)
-    ys = [lax.rem(gy + o, 8) for o in range(1, 8)]
-    zs = [lax.rem(gz + o, 4) for o in range(1, 4)]
+    ys = [lax.rem(gy + o, 8) for o in range(8)]
+    zs = [lax.rem(gz + o, 4) for o in range(4)]
+    near = [(dx, o) for dx in range(2) for o in range(8) if dx + o > 0]
+    side = lambda dx: gx + dx * (2 - 4 * xh)
+    half = lambda dx: xh + dx * (1 - 2 * xh)
     second = (
-        [send(d1.at[:, y], r2y.at[n], {"gy": y}, 8 + n) for n, y in enumerate(ys)],
-        [send(d1.at[:, :, z], r2z.at[n], {"gz": z}, 15 + n) for n, z in enumerate(zs)],
+        [send(d1.at[:, ys[o]], r2y.at[o - 1], {"gy": ys[o]}, 6 + o) for o in range(1, 8)],
+        [send(d1.at[:, :, zs[o]], r2z.at[o - 1], {"gz": zs[o]}, 13 + o) for o in range(1, 4)],
     )
     third = (
-        [send(s2y.at[:, z], r3z.at[n], {"gz": z}, 18 + n) for n, z in enumerate(zs)],
-        [send(s2z.at[:, y], r3y.at[n], {"gy": y}, 21 + n) for n, y in enumerate(ys)],
+        [
+            send(s2y.at[half(dx), zs[o]], r3z.at[n], {"gx": side(dx), "gz": zs[o]}, 17 + n)
+            for n, (dx, o) in enumerate([p for p in near if p[1] < 4])
+        ],
+        [
+            send(s2z.at[half(dx), ys[o]], r3y.at[n], {"gx": side(dx), "gy": ys[o]}, 24 + n)
+            for n, (dx, o) in enumerate(near)
+        ],
     )
     for way in range(2):
         @pl.when(core == way)
@@ -737,35 +759,32 @@
                 s2z[x, h] = acc
         each(third[1], "start")
 
-    lax.fori_loop(16, 24, plane, 0)
+    lax.fori_loop(16, CX, plane, 0)
+    store.append(pltpu.make_async_copy(fb.at[16:32], out.at[16:32], lsem.at[8]))
+    store[1].start()
+
     @pl.when(core == 0)
     def _():
         each(third[0], "wait_recv")
-        for x in range(2):
-            acc = s2y[x, gz]
-            for o in range(3):
-                acc = acc + r3z[o, x]
-            s3[x] = acc
-        each(second[0], "wait_send")
-        each(third[0], "wait_send")
+        acc = s2y[xh, gz]
+        for n in range(7):
+            acc = acc + r3z[n]
+        grad[...] = acc
 
     @pl.when(core == 1)
     def _():
         each(third[1], "wait_recv")
-        for x in range(2):
-            acc = s2z[x, gy]
-            for o in range(7):
-                acc = acc + r3y[o, x]
-            s3[x] = acc
-        each(second[1], "wait_send")
-        each(third[1], "wait_send")
-
-    last = send(s3.at[1 - xh], r4, {"gx": gx + 2 - 4 * xh})
-    lax.fori_loop(24, CX, plane, 0)
-    store.append(pltpu.make_async_copy(fb.at[16:32], out.at[16:32], lsem.at[8]))
-    store[1].start()
-    last.wait_recv()
-    grad[...] = s3[xh] + r4[...]
+        acc = s2z[xh, gy]
+        for n in range(15):
+            acc = acc + r3y[n]
+        grad[...] = acc
+
+    for way in range(2):
+        @pl.when(core == way)
+        def _():
+            each(second[way], "wait_send")
+            each(third[way], "wait_send")
+
     for copy in started:
         copy.wait_send()
     for copy in store:
@@ -791,15 +810,32 @@
             pltpu.VMEM((2, 8, 4, 16, 128), f32), pltpu.VMEM((2, 8, 4, 16, 128), f32),
             pltpu.VMEM((7, 2, 4, 16, 128), f32), pltpu.VMEM((3, 2, 8, 16, 128), f32),
             pltpu.VMEM((2, 4, 16, 128), f32), pltpu.VMEM((2, 8, 16, 128), f32),
-            pltpu.VMEM((3, 2, 16, 128), f32), pltpu.VMEM((7, 2, 16, 128), f32),
-            pltpu.VMEM((2, 16, 128), f32), pltpu.VMEM((16, 128), f32),
-            pltpu.SemaphoreType.DMA((9,)), pltpu.SemaphoreType.DMA((28,)),
-            pltpu.SemaphoreType.DMA((28,)),
+            pltpu.VMEM((7, 16, 128), f32), pltpu.VMEM((15, 16, 128), f32),
+            pltpu.SemaphoreType.DMA((9,)), pltpu.SemaphoreType.DMA((39,)),
+            pltpu.SemaphoreType.DMA((39,)),
         ],
         compiler_params=pltpu.CompilerParams(
             collective_id=1, has_side_effects=True, vmem_limit_bytes=62 << 20
         ),
     )(adj1, base, solid, vx, vy, vz, dense, ly, lz, cx, cy, cz)
+
+
+def hand_on_kernel(start_ref, grad_ref, start_out, grad_out):
+    start_out[...] = start_ref[...]
+    grad_out[...] = grad_ref[...]
+
+
+def hand_on(start, grad):
+    some = pl.BlockSpec((8, CY, CZ), lambda i: (i, 0, 0))
+    small = pl.BlockSpec((16, 128), lambda i: (0, 0))
+    return pl.pallas_call(
+        hand_on_kernel,
+        out_shape=(jax.ShapeDtypeStruct(start.shape, f32), jax.ShapeDtypeStruct(grad.shape, f32)),
+        grid=(CX // 8,),
+        in_specs=[some, small],
+        out_specs=(some, small),
+        compiler_params=pltpu.CompilerParams(vmem_limit_bytes=62 << 20),
+    )(start, grad)
 
 
 def per_device(
@@ -814,6 +850,7 @@
     start, grad = call_finish(
         adj1, base, solid, vel_x, vel_y, vel_z, dense.reshape(2, 2, 8, 4, 16, 128), ly, lz, cx, cy, cz
     )
+    start, grad = hand_on(start, grad)
     return start, load_start, grad.reshape(2048)
 
 

time: 106 us -> 106 us (level)
  local copies, waits for them, and re-layouts: 3.74 us -> 0 us
  Pallas kernels: 102 us -> 105 us
    pallas_call x0 -> x1, Pallas kernels: none -> 3.79 us  [hand_on(): pl.pallas_call(hand_on_kernel, out_shape=(jax.ShapeDtypeStruct(start.shap...]
    unnamed x4 -> x0, local copies, waits for them, and re-layouts: 3.74 us -> none
where the time goes in v5:
time: 106 us; the launch traced here: 105 us
  Pallas kernels  105 us (99%)
    pallas_call x1, Pallas kernels, call_main(): pl.pallas_call(main_kernel, out_shape=[jax.ShapeDtypeStruct(s, f32) for s...  51 us
    pallas_call x1, Pallas kernels, call_faces(): pl.pallas_call(gather_faces, out_shape=outs, in_specs=[ANY] * 7, out_spec...  29.7 us
    pallas_call x1, Pallas kernels, call_finish(): pl.pallas_call(finish_kernel, out_shape=(jax.ShapeDtypeStruct((CX, CY, CZ...  20.2 us
    pallas_call x1, Pallas kernels, hand_on(): pl.pallas_call(hand_on_kernel, out_shape=(jax.ShapeDtypeStruct(start.shap...  3.79 us

profile of v5, /device:TPU:1, one launch (start us, length us, event | category | flops | bytes accessed | tf_op | source)
XLA Modules:
  0.0 105.4 jit_solution(15848103544712628900)
XLA Ops:
  0.6 29.7 %shard_map.139 = (f32[3,64,256]{2,1,0:T(8,128)}, s32[64,256]{1,0:T(8,128)}, f32[2,64,256]{2,1,0:T(8,128)}, s32[64,256]{1,0:T(8,128)}, f32[4,32,256]{2,1,0:T(8,12...) custom-call(f32[32,64,256]{2,1,0:T(8,128)} %conc_ref.1, ...), custom_call_target="tpu_custom_call" | custom-call | tf_op jit(solution)/shard_map/pallas_call | solution.py:252
  30.4 51.0 %shard_map.140 = (f32[32,64,256]{2,1,0:T(8,128)}, f32[32,64,256]{2,1,0:T(8,128)}, f32[32,64,256]{2,1,0:T(8,128)}, f32[2048,128]{1,0:T(8,128)}, f32[2,32,256]{2,1...) custom-call(s32[1]{0:T(128)} %bitcast.block_ref, ...), custom_call_target="tpu_custom_call" | custom-call | flops 1000000000 | bytes 26214400 | tf_op jit(solution)/shard_map/pallas_call | solution.py:591
  81.4 20.2 %shard_map.141 = (f32[32,64,256]{2,1,0:T(8,128)}, f32[16,128]{1,0:T(8,128)}) custom-call(f32[32,64,256]{2,1,0:T(8,128)} %get-tuple-element.46.adj1, f32[32,64,256]{2,1,0:T(8,128)} %get-tuple-element.47.base, s32[32,64,256]{2,1,0:T(8,128)} %solid.3, f32[32,64,256]{2,1,0:T(8,128)} %vx.3, f32[32,64,256]{2,1,0:T(8,128)} %vy.3, f32[32,64,256]{2,1,0:T(8,128)} %vz.3, ...), custom_call_target="tpu_custom_call" | custom-call | tf_op jit(solution)/shard_map/pallas_call | solution.py:797
  101.6 3.8 %shard_map.142 = (f32[32,64,256]{2,1,0:T(8,128)}, f32[16,128]{1,0:T(8,128)}) custom-call(f32[32,64,256]{2,1,0:T(8,128)} %get-tuple-element.54.start_ref, f32[16,128]{1,0:T(8,128)} %get-tuple-element.55.grad_ref), custom_call_target="tpu_custom_call" | custom-call | tf_op jit(solution)/shard_map/pallas_call | solution.py:831

commit v6 on v5

--- a/solution.py
+++ b/solution.py
@@ -10,7 +10,7 @@
 f32, bf16, i32, f8 = jnp.float32, jnp.bfloat16, jnp.int32, jnp.float8_e4m3fn
 DIGITS = 3
 CHUNKS = 4
-PLANES = 2
+PLANES = 4
 MESH = pl.DeviceIdType.MESH
 ANY = pl.BlockSpec(memory_space=pl.ANY)
 dispersion = 0.06
@@ -820,20 +820,38 @@
     )(adj1, base, solid, vx, vy, vz, dense, ly, lz, cx, cy, cz)
 
 
-def hand_on_kernel(start_ref, grad_ref, start_out, grad_out):
-    start_out[...] = start_ref[...]
-    grad_out[...] = grad_ref[...]
+PARTS = 8
+
+
+def hand_on_kernel(start, grad, start_out, grad_out, buf, in_sem, out_sem):
+    size = CX // PARTS
+    small = pltpu.make_async_copy(grad, grad_out, in_sem.at[PARTS])
+    small.start()
+    parts = [pl.ds(size * q, size) for q in range(PARTS)]
+    ins = [pltpu.make_async_copy(start.at[p], buf.at[p], in_sem.at[q]) for q, p in enumerate(parts)]
+    outs = [
+        pltpu.make_async_copy(buf.at[p], start_out.at[p], out_sem.at[q]) for q, p in enumerate(parts)
+    ]
+    for copy in ins:
+        copy.start()
+    for q in range(PARTS):
+        ins[q].wait()
+        outs[q].start()
+    for copy in outs:
+        copy.wait()
+    small.wait()
 
 
 def hand_on(start, grad):
-    some = pl.BlockSpec((8, CY, CZ), lambda i: (i, 0, 0))
-    small = pl.BlockSpec((16, 128), lambda i: (0, 0))
     return pl.pallas_call(
         hand_on_kernel,
         out_shape=(jax.ShapeDtypeStruct(start.shape, f32), jax.ShapeDtypeStruct(grad.shape, f32)),
-        grid=(CX // 8,),
-        in_specs=[some, small],
-        out_specs=(some, small),
+        in_specs=[ANY] * 2,
+        out_specs=[ANY] * 2,
+        scratch_shapes=[
+            pltpu.VMEM((CX, CY, CZ), f32), pltpu.SemaphoreType.DMA((PARTS + 1,)),
+            pltpu.SemaphoreType.DMA((PARTS,)),
+        ],
         compiler_params=pltpu.CompilerParams(vmem_limit_bytes=62 << 20),
     )(start, grad)
 

time: 106 us -> 103 us (0.972)
  Pallas kernels: 105 us -> 102 us
    pallas_call x1, Pallas kernels: 3.79 us -> 2.41 us  [hand_on(): pl.pallas_call(hand_on_kernel, out_shape=(jax.ShapeDtypeStruct(start.shap...]
where the time goes in v6:
time: 103 us
  Pallas kernels  102 us (99%)
    pallas_call x1, Pallas kernels, call_main(): pl.pallas_call(main_kernel, out_shape=[jax.ShapeDtypeStruct(s, f32) for s...  50.1 us
    pallas_call x1, Pallas kernels, call_faces(): pl.pallas_call(gather_faces, out_shape=outs, in_specs=[ANY] * 7, out_spec...  29.7 us
    pallas_call x1, Pallas kernels, call_finish(): pl.pallas_call(finish_kernel, out_shape=(jax.ShapeDtypeStruct((CX, CY, CZ...  20.2 us
    pallas_call x1, Pallas kernels, hand_on(): pl.pallas_call(hand_on_kernel, out_shape=(jax.ShapeDtypeStruct(start.shap...  2.41 us

profile of v6, /device:TPU:1, one launch (start us, length us, event | category | flops | bytes accessed | tf_op | source)
XLA Modules:
  0.0 103.1 jit_solution(18392212209705361025)
XLA Ops:
  0.6 29.7 %shard_map.139 = (f32[3,64,256]{2,1,0:T(8,128)}, s32[64,256]{1,0:T(8,128)}, f32[2,64,256]{2,1,0:T(8,128)}, s32[64,256]{1,0:T(8,128)}, f32[4,32,256]{2,1,0:T(8,12...) custom-call(f32[32,64,256]{2,1,0:T(8,128)} %conc_ref.1, ...), custom_call_target="tpu_custom_call" | custom-call | tf_op jit(solution)/shard_map/pallas_call | solution.py:252
  30.4 50.1 %shard_map.140 = (f32[32,64,256]{2,1,0:T(8,128)}, f32[32,64,256]{2,1,0:T(8,128)}, f32[32,64,256]{2,1,0:T(8,128)}, f32[2048,128]{1,0:T(8,128)}, f32[2,32,256]{2,1...) custom-call(s32[1]{0:T(128)} %bitcast.block_ref, ...), custom_call_target="tpu_custom_call" | custom-call | flops 1000000000 | bytes 26214400 | tf_op jit(solution)/shard_map/pallas_call | solution.py:591
  80.5 20.2 %shard_map.141 = (f32[32,64,256]{2,1,0:T(8,128)}, f32[16,128]{1,0:T(8,128)}) custom-call(f32[32,64,256]{2,1,0:T(8,128)} %get-tuple-element.46.adj1, f32[32,64,256]{2,1,0:T(8,128)} %get-tuple-element.47.base, s32[32,64,256]{2,1,0:T(8,128)} %solid.3, f32[32,64,256]{2,1,0:T(8,128)} %vx.3, f32[32,64,256]{2,1,0:T(8,128)} %vy.3, f32[32,64,256]{2,1,0:T(8,128)} %vz.3, ...), custom_call_target="tpu_custom_call" | custom-call | tf_op jit(solution)/shard_map/pallas_call | solution.py:797
  100.7 2.4 %shard_map.142 = (f32[32,64,256]{2,1,0:T(8,128)}, f32[16,128]{1,0:T(8,128)}) custom-call(f32[32,64,256]{2,1,0:T(8,128)} %get-tuple-element.54.start, f32[16,128]{1,0:T(8,128)} %get-tuple-element.55.grad), custom_call_target="tpu_custom_call" | custom-call | tf_op jit(solution)/shard_map/pallas_call | solution.py:846

commit v7 on v6

--- a/solution.py
+++ b/solution.py
@@ -169,6 +169,12 @@
         s1[x] = div + flux - down_z(flux)
         d = up_z(l) - l
         s2[x] = lap + b * d - down_z(a * d)
+        return carry
+
+    def edges(x, carry):
+        lane = lax.broadcasted_iota(i32, (CY, 128), 1)
+        at = pl.ds(x, 1)
+        c, l, w, v_y, v_z = cb[x], lb[x], weight_of(sb[x]), vyb[x], vzb[x]
         for k, v in enumerate((c, l, v_y, w)):
             yfwd[k, at, :] = v[CY - 1:CY, :]
         for k, v in enumerate((c, l, w)):
@@ -188,18 +194,20 @@
             copy.wait()
 
     mine.wait()
-    arrived(0)
-    arrived(1)
-    lax.fori_loop(0, 5, plane, 0)
+    for q in range(4):
+        arrived(q)
+    lax.fori_loop(0, CX, edges, 0)
+    faces.append(send(yfwd, ylo, {"gy": lax.rem(gy + 1, 8)}))
+    faces.append(send(ybwd, yhi, {"gy": lax.rem(gy + 7, 8)}))
+    faces.append(send(zfwd, zlo, {"gz": lax.rem(gz + 1, 4)}))
+    faces.append(send(zbwd, zhi, {"gz": lax.rem(gz + 3, 4)}))
     for way in range(2):
         @pl.when(core == way)
         def _():
             each(second[way], "wait_recv")
             each(third[way], "start")
 
-    arrived(2)
-    arrived(3)
-    lax.fori_loop(5, 24, plane, 0)
+    lax.fori_loop(0, 24, plane, 0)
     for way in range(2):
         @pl.when(core == way)
         def _():
@@ -215,10 +223,6 @@
     for copy in outs:
         copy.start()
     lax.fori_loop(24, CX, plane, 0)
-    faces.append(send(yfwd, ylo, {"gy": lax.rem(gy + 1, 8)}))
-    faces.append(send(ybwd, yhi, {"gy": lax.rem(gy + 7, 8)}))
-    faces.append(send(zfwd, zlo, {"gz": lax.rem(gz + 1, 4)}))
-    faces.append(send(zbwd, zhi, {"gz": lax.rem(gz + 3, 4)}))
     keep = [
         pltpu.make_async_copy(s1.at[24:32], s1_out.at[24:32], osem.at[3]),
         pltpu.make_async_copy(s2.at[24:32], s2_out.at[24:32], osem.at[4]),

time: 103 us -> 99.6 us (0.967)
  Pallas kernels: 102 us -> 98.8 us
    pallas_call x1, Pallas kernels: 29.7 us -> 26.1 us  [call_faces(): pl.pallas_call(gather_faces, out_shape=outs, in_specs=[ANY] * 7, out_spec...]
where the time goes in v7:
time: 99.6 us; the launch traced here: 99.5 us
  Pallas kernels  98.8 us (99%)
    pallas_call x1, Pallas kernels, call_main(): pl.pallas_call(main_kernel, out_shape=[jax.ShapeDtypeStruct(s, f32) for s...  50.1 us
    pallas_call x1, Pallas kernels, call_faces(): pl.pallas_call(gather_faces, out_shape=outs, in_specs=[ANY] * 7, out_spec...  26.1 us
    pallas_call x1, Pallas kernels, call_finish(): pl.pallas_call(finish_kernel, out_shape=(jax.ShapeDtypeStruct((CX, CY, CZ...  20.2 us
    pallas_call x1, Pallas kernels, hand_on(): pl.pallas_call(hand_on_kernel, out_shape=(jax.ShapeDtypeStruct(start.shap...  2.41 us

profile of v7, /device:TPU:1, one launch (start us, length us, event | category | flops | bytes accessed | tf_op | source)
XLA Modules:
  0.0 99.5 jit_solution(7722208617447256738)
XLA Ops:
  0.6 26.1 %shard_map.139 = (f32[3,64,256]{2,1,0:T(8,128)}, s32[64,256]{1,0:T(8,128)}, f32[2,64,256]{2,1,0:T(8,128)}, s32[64,256]{1,0:T(8,128)}, f32[4,32,256]{2,1,0:T(8,12...) custom-call(f32[32,64,256]{2,1,0:T(8,128)} %conc_ref.1, ...), custom_call_target="tpu_custom_call" | custom-call | tf_op jit(solution)/shard_map/pallas_call | solution.py:256
  26.8 50.1 %shard_map.140 = (f32[32,64,256]{2,1,0:T(8,128)}, f32[32,64,256]{2,1,0:T(8,128)}, f32[32,64,256]{2,1,0:T(8,128)}, f32[2048,128]{1,0:T(8,128)}, f32[2,32,256]{2,1...) custom-call(s32[1]{0:T(128)} %bitcast.block_ref, ...), custom_call_target="tpu_custom_call" | custom-call | flops 1000000000 | bytes 26214400 | tf_op jit(solution)/shard_map/pallas_call | solution.py:595
  76.9 20.2 %shard_map.141 = (f32[32,64,256]{2,1,0:T(8,128)}, f32[16,128]{1,0:T(8,128)}) custom-call(f32[32,64,256]{2,1,0:T(8,128)} %get-tuple-element.46.adj1, f32[32,64,256]{2,1,0:T(8,128)} %get-tuple-element.47.base, s32[32,64,256]{2,1,0:T(8,128)} %solid.3, f32[32,64,256]{2,1,0:T(8,128)} %vx.3, f32[32,64,256]{2,1,0:T(8,128)} %vy.3, f32[32,64,256]{2,1,0:T(8,128)} %vz.3, ...), custom_call_target="tpu_custom_call" | custom-call | tf_op jit(solution)/shard_map/pallas_call | solution.py:801
  97.1 2.4 %shard_map.142 = (f32[32,64,256]{2,1,0:T(8,128)}, f32[16,128]{1,0:T(8,128)}) custom-call(f32[32,64,256]{2,1,0:T(8,128)} %get-tuple-element.54.start, f32[16,128]{1,0:T(8,128)} %get-tuple-element.55.grad), custom_call_target="tpu_custom_call" | custom-call | tf_op jit(solution)/shard_map/pallas_call | solution.py:850
